TPU v7x, 512 devices: a whole 4x4x16 slice. The times are simulated.
512 devices in a mesh: pair: 64 (over z, y), tile: 8 (over x, core).
Axes of the slice: x: 4, y: 4, z: 16, core: 2. Of those that a mesh axis runs over, the one named last changes fastest.
Arguments:
- candidates: bfloat16 [131072, 768], P(('pair', 'tile')), may hold values from -12 to 12, as said below
- validation: bfloat16 [8192, 768], P('tile'), may hold values from -12 to 12, as said below
- row_sizes: int32 [16], replicated, may hold values from 1024 to 24576, as said below
- col_sizes: int32 [16], replicated, may hold values from 1 to 1536, 8192 in all
Outputs:
- row_value: float32 [131072], P(('pair', 'tile'))
- col_potential: float32 [8192], P('tile')
Inputs may be any that keep to these rules, and one draw needn't show every extreme that they name: `candidates`: each row's entries are drawn alike and scaled by one factor of the row. `validation`: each row's entries are drawn alike and scaled by one factor of the row. `row_sizes`: every domain pair has 1024 rows or more; one pair has exactly 1024 rows and one exactly 24576.
All inputs are finite; a program needn't handle non-finite values.
Results may differ from a plain program's by a relative error of at most 0.0003.
Values may be sent and summed in bfloat16 or wider, within the bound.
A program may use at most 192 MiB of HBM per device.

v0:
```python
import jax
import jax.numpy as jnp
from jax import lax
from jax.sharding import PartitionSpec as P

ITERS = 3


EPS = 0.02
NEG = -1e30


def combined_all(value, axis, combine):
    everything = jax.tree.map(lambda part: lax.all_gather(part, axis), value)
    first = jax.tree.map(lambda part: part[0], everything)

    def lap(k, so_far):
        return combine(so_far, jax.tree.map(lambda part: part[k], everything))

    return lax.fori_loop(1, lax.axis_size(axis), lap, first)


def combine_pair(first, second):
    top = jnp.maximum(first[0], second[0])
    return (top, first[1] * jnp.exp(first[0] - top) + second[1] * jnp.exp(second[0] - top))


def pair_index(positions, sizes):
    ends = jnp.cumsum(sizes)
    return jnp.sum((positions[:, None] >= ends[None, :]).astype(jnp.int32), axis=1)


def one_hot(pairs, count):
    return (pairs[:, None] == jnp.arange(count, dtype=jnp.int32)[None, :]).astype(jnp.float32)


def lookup(hot, table):
    return jnp.dot(hot, table, precision=lax.Precision.HIGHEST)


def cost_block(rows, columns):
    rows_f = rows.astype(jnp.float32)
    cols_f = columns.astype(jnp.float32)
    row_norm = jnp.sum(rows_f * rows_f, axis=1)
    col_norm = jnp.sum(cols_f * cols_f, axis=1)
    cross = lax.dot_general(
        rows, columns, (((1,), (1,)), ((), ())), preferred_element_type=jnp.float32
    )
    return (row_norm[:, None] + col_norm[None, :] - 2.0 * cross) / rows.shape[1]


def row_stats(cost, mask, potential):
    scores = jnp.where(mask, (potential[None, :] - cost) / EPS, NEG)
    top = jnp.max(scores, axis=1)
    total = jnp.sum(jnp.where(mask, jnp.exp(scores - top[:, None]), 0.0), axis=1)
    return (top, total)


def col_stats(cost, mask, potential):
    scores = jnp.where(mask, (potential[:, None] - cost) / EPS, NEG)
    top = jnp.max(scores, axis=0)
    total = jnp.sum(jnp.where(mask, jnp.exp(scores - top[None, :]), 0.0), axis=0)
    return (top, total)


def local(candidates, validation, row_sizes, col_sizes):
    tile_count = lax.axis_size("tile")
    tile_place = lax.axis_index("tile")
    pair_place = lax.axis_index("pair")
    row_dev = candidates.shape[0]
    col_dev = validation.shape[0]
    pair_count = row_sizes.shape[0]
    row_table = EPS * jnp.log(row_sizes.astype(jnp.float32))
    col_table = EPS * jnp.log(col_sizes.astype(jnp.float32))
    inverse_rows = 1.0 / row_sizes.astype(jnp.float32)
    cost = cost_block(lax.all_gather(candidates, "tile", axis=0, tiled=True), validation)
    group_rows = row_dev * tile_count
    row_pos = pair_place * group_rows + jnp.arange(group_rows, dtype=jnp.int32)
    col_pos = tile_place * col_dev + jnp.arange(col_dev, dtype=jnp.int32)
    row_pair = pair_index(row_pos, row_sizes)
    col_pair = pair_index(col_pos, col_sizes)
    mask = row_pair[:, None] == col_pair[None, :]
    row_hot = one_hot(row_pair, pair_count)
    col_hot = one_hot(col_pair, pair_count)
    row_shift = lookup(row_hot, col_table)
    col_shift = lookup(col_hot, row_table)
    potential_g = jnp.zeros((col_dev,), jnp.float32)
    for step in range(ITERS):
        top, total = row_stats(cost, mask, potential_g)
        top, total = combined_all((top, total), "tile", combine_pair)
        potential_f = -EPS * (top + jnp.log(total)) + row_shift
        top, total = col_stats(cost, mask, potential_f)
        if step + 1 < ITERS:
            top, total = combined_all((top, total), "pair", combine_pair)
        else:
            partial_value = jnp.dot(potential_f, row_hot, precision=lax.Precision.HIGHEST)
            top, total = combined_all((top, total), "pair", combine_pair)
            sums = lax.psum(partial_value, "pair")
        potential_g = -EPS * (top + jnp.log(total)) + col_shift
    own_f = lax.dynamic_slice_in_dim(potential_f, tile_place * row_dev, row_dev)
    own_hot = lax.dynamic_slice_in_dim(row_hot, tile_place * row_dev, row_dev)
    means = sums * inverse_rows
    row_value = own_f - lookup(own_hot, means)
    return (row_value, potential_g)


def solution(mesh):
    in_specs = (P(("pair", "tile"), None), P("tile", None), P(), P())
    out_specs = (P(("pair", "tile")), P("tile"))
    return jax.shard_map(local, mesh=mesh, in_specs=in_specs, out_specs=out_specs, check_vma=False)
```

profile of v0, /device:TPU:2, one launch (start us, length us, event | category | flops | bytes accessed | tf_op | source)
XLA Modules:
  0.0 835.7 jit_solution(1296715752073679391)
XLA Ops:
  7.2 0.7 all-gather.14.cloned.1.call-update
  7.9 0.7 copy.12
  8.7 0.1 reduce
  8.8 0.7 copy.13
  9.6 0.1 reduce.1
  9.9 1.8 multiply_reduce_fusion.1
  11.7 1.1 fusion.15
  12.8 1.4 fusion.12
  14.2 0.4 iota_compare_fusion
  14.5 34.4 %all-gather.14.cloned.1.call-done = bf16[2048,768]{1,0:T(8,128)(2,1)} async-done(((bf16[256,768]{1,0:T(8,128)(2,1)}), bf16[2048,768]{1,0:T(8,128)(2,1)}) %all-gather.14.cloned.1.call-update) | async-done | bytes 3145744 | tf_op jit(solution)/shard_map/all_gather | solution.py:76
  49.0 2.6 multiply_reduce_fusion
  51.5 7.1 fusion.6
  58.7 3.2 copy-done
  61.9 2.7 fusion
  64.6 12.7 %all-gather.1 = f32[16384]{0:T(1024)S(1)} all-gather(f32[2048]{0:T(1024)S(1)} %fusion), channel_id=3, replica_groups=mesh['pair'=64,'tile'=8] {'tile'}, dimensions={0}, use_global_device_ids=true | all-gather | bytes 73728 | tf_op jit(solution)/shard_map/all_gather | solution.py:14
  77.4 12.8 %all-gather = f32[16384]{0:T(1024)S(1)} all-gather(f32[2048]{0:T(1024)S(1)} %get-tuple-element.896), channel_id=2, replica_groups=mesh['pair'=64,'tile'=8] {'tile'}, dimensions={0}, use_global_device_ids=true | all-gather | bytes 73728 | tf_op jit(solution)/shard_map/all_gather | solution.py:14
  90.1 0.5 while.102
  90.6 4.5 fusion.7
  95.1 1.3 copy-done.1
  96.4 3.1 fusion.1
  99.6 83.8 %all-gather.3 = f32[65536]{0:T(1024)S(1)} all-gather(f32[1024]{0:T(1024)S(1)} %fusion.1), channel_id=5, replica_groups=mesh['pair'=64,'tile'=8] {'pair'}, dimensions={0}, use_global_device_ids=true | all-gather | bytes 266240 | tf_op jit(solution)/shard_map/all_gather | solution.py:14
  183.4 80.8 %all-gather.2 = f32[65536]{0:T(1024)S(1)} all-gather(f32[1024]{0:T(1024)S(1)} %fusion.7), channel_id=4, replica_groups=mesh['pair'=64,'tile'=8] {'pair'}, dimensions={0}, use_global_device_ids=true | all-gather | bytes 266240 | tf_op jit(solution)/shard_map/all_gather | solution.py:14
  264.3 3.7 while.103
  268.0 4.3 fusion.8
  272.3 5.0 fusion.2
  277.3 12.8 %all-gather.5 = f32[16384]{0:T(1024)S(1)} all-gather(f32[2048]{0:T(1024)S(1)} %fusion.2), channel_id=7, replica_groups=mesh['pair'=64,'tile'=8] {'tile'}, dimensions={0}, use_global_device_ids=true | all-gather | bytes 73728 | tf_op jit(solution)/shard_map/all_gather | solution.py:14
  290.1 12.8 %all-gather.4 = f32[16384]{0:T(1024)S(1)} all-gather(f32[2048]{0:T(1024)S(1)} %fusion.8), channel_id=6, replica_groups=mesh['pair'=64,'tile'=8] {'tile'}, dimensions={0}, use_global_device_ids=true | all-gather | bytes 73728 | tf_op jit(solution)/shard_map/all_gather | solution.py:14
  302.9 0.5 while.104
  303.4 4.2 fusion.9
  307.6 4.8 fusion.3
  312.4 79.9 %all-gather.7 = f32[65536]{0:T(1024)S(1)} all-gather(f32[1024]{0:T(1024)S(1)} %fusion.3), channel_id=9, replica_groups=mesh['pair'=64,'tile'=8] {'pair'}, dimensions={0}, use_global_device_ids=true | all-gather | bytes 266240 | tf_op jit(solution)/shard_map/all_gather | solution.py:14
  392.4 80.8 %all-gather.6 = f32[65536]{0:T(1024)S(1)} all-gather(f32[1024]{0:T(1024)S(1)} %fusion.9), channel_id=8, replica_groups=mesh['pair'=64,'tile'=8] {'pair'}, dimensions={0}, use_global_device_ids=true | all-gather | bytes 266240 | tf_op jit(solution)/shard_map/all_gather | solution.py:14
  473.2 3.7 while.105
  477.0 4.3 fusion.10
  481.3 5.0 fusion.4
  486.3 12.8 %all-gather.9 = f32[16384]{0:T(1024)S(1)} all-gather(f32[2048]{0:T(1024)S(1)} %fusion.4), channel_id=11, replica_groups=mesh['pair'=64,'tile'=8] {'tile'}, dimensions={0}, use_global_device_ids=true | all-gather | bytes 73728 | tf_op jit(solution)/shard_map/all_gather | solution.py:14
  499.1 13.0 %all-gather.8 = f32[16384]{0:T(1024)S(1)} all-gather(f32[2048]{0:T(1024)S(1)} %fusion.10), channel_id=10, replica_groups=mesh['pair'=64,'tile'=8] {'tile'}, dimensions={0}, use_global_device_ids=true | all-gather | bytes 73728 | tf_op jit(solution)/shard_map/all_gather | solution.py:14
  512.1 0.5 while.106
  512.6 4.2 fusion.11
  516.8 4.8 fusion.5
  521.7 79.9 %all-gather.11 = f32[65536]{0:T(1024)S(1)} all-gather(f32[1024]{0:T(1024)S(1)} %fusion.5), channel_id=13, replica_groups=mesh['pair'=64,'tile'=8] {'pair'}, dimensions={0}, use_global_device_ids=true | all-gather | bytes 266240 | tf_op jit(solution)/shard_map/all_gather | solution.py:14
  601.6 80.8 %all-gather.10 = f32[65536]{0:T(1024)S(1)} all-gather(f32[1024]{0:T(1024)S(1)} %fusion.11), channel_id=12, replica_groups=mesh['pair'=64,'tile'=8] {'pair'}, dimensions={0}, use_global_device_ids=true | all-gather | bytes 266240 | tf_op jit(solution)/shard_map/all_gather | solution.py:14
  682.5 0.6 convolution_bitcast_fusion
  683.0 3.7 while.107
  686.8 140.6 %psum.7 = f32[16]{0:T(128)S(1)} all-reduce(f32[16]{0:T(128)S(1)} %convolution_bitcast_fusion), channel_id=1, replica_groups=mesh['pair'=64,'tile'=8] {'pair'}, use_global_device_ids=true, to_apply=%region_26.27 | all-reduce | flops 16 | bytes 128 | tf_op jit(solution)/shard_map/psum | solution.py:98
  827.4 0.1 fusion.17
  827.5 0.7 dynamic-slice_subtract_fusion
  828.2 0.6 multiply_add_fusion.9
  (460 shorter events, 6.4 us)
Async XLA Ops:
  7.2 41.8 %all-gather.14.cloned.1.call-start = ((), (), s32[]{:S(2)}) async-start(), calls=%async_computation | async-start | bytes 3538944 | tf_op jit(solution)/shard_map/all_gather | solution.py:76
  58.7 3.2 copy-start
  90.6 5.8 copy-start.1
  512.6 314.8 %copy-start.2 = (s32[16]{0:T(128)S(1)}, s32[16]{0:T(128)}, u32[]{:S(2)}) copy-start(s32[16]{0:T(128)} %param.18) | copy-start | bytes 196
Sparse Core Ops, SparseCore 0:
  10.1 38.8 all-gather.13
where the time goes:
time: 836 us
  blocking collectives  703 us (84%)
  other arithmetic  56 us (7%)
  waiting for transfers between devices  35.1 us (4%)
  between operations  14.4 us (2%)
  matrix products  10.3 us (1%)
  local copies, waits for them, and re-layouts  9.55 us (1%)
    all_gather x12, blocking collectives, combined_all(): everything = jax.tree.map(lambda part: lax.all_gather(part, axis), value)  563 us
    psum x1, blocking collectives, local(): sums = lax.psum(partial_value, 'pair')  141 us
    all_gather x1, waiting for transfers between devices, local(): lax.all_gather(candidates, 'tile', axis=0, tiled=True)  34.4 us
  transfers between devices with their start and end apart: 1, of which 1 were waited for; matrix products, arithmetic and copies ran while one was open for 1% of the time, Pallas kernels for 0%

commit v1 on v0

v1 whole, which is shorter than its diff:
```python
import functools
import math

import jax
import jax.numpy as jnp
from jax import lax
from jax.experimental import pallas as pl
from jax.experimental.pallas import tpu as pltpu
from jax.sharding import PartitionSpec as P

ITERS = 3
EPS = 0.02
NEG = -1e30
EMPTY = -1e29
LOG2E = math.log2(math.e)
NX, NY = 4, 4
TILES = 2 * NX
ROW_MOST = 24576
LANES = 128
MESH = pl.DeviceIdType.MESH


def pair_of(position, ends):
    pair = jnp.zeros(position.shape, jnp.int32)
    for end in ends:
        pair += (position >= end).astype(jnp.int32)
    return pair


def size_of(pair, sizes):
    size = jnp.zeros(pair.shape, jnp.float32)
    for k, s in enumerate(sizes):
        size = jnp.where(pair == k, s.astype(jnp.float32), size)
    return size


def merged(parts):
    top = jnp.max(parts, axis=0)
    return top + jnp.log2(jnp.sum(jnp.exp2(parts - top[None]), axis=0))


def kernel(
    pair_count,
    group_count,
    rs_ref,
    cs_ref,
    x_ref,
    y_ref,
    f_ref,
    g_ref,
    rows,
    scores,
    v_wide,
    pair_wide,
    top_wide,
    cn,
    column,
    row_box,
    y_box,
    z_box,
    local_sem,
    send_sem,
    block_sem,
    row_sem,
    y_sem,
    z_sem,
):
    n_row, depth = x_ref.shape
    n_col = y_ref.shape[0]
    half = n_row // 2
    halves = 2 * TILES
    col_blocks = n_col // LANES
    nz = group_count // NY
    window = min(-(-ROW_MOST // (n_row * TILES * NY)), nz // 2)
    scale = 2.0 * LOG2E / (depth * EPS)
    shift = LOG2E / (depth * EPS)

    group = lax.axis_index("pair")
    tile = lax.axis_index("tile")
    z, y = group // NY, lax.rem(group, NY)
    x, core = tile // 2, lax.rem(tile, 2)

    def at(dx, flip):
        other = 1 - core if flip else core
        return 2 * lax.rem(x + dx, NX) + other

    def in_y(r):
        return z * NY + lax.rem(y + r, NY)

    def in_z(r):
        return lax.rem(z + r, nz) * NY + y

    with jax.named_scope("greet"):
        own_copy = pltpu.make_async_copy(x_ref, rows.at[tile], local_sem)
        own_copy.start()
        barrier = pltpu.get_barrier_semaphore()
        for r in range(1, TILES):
            pl.semaphore_signal(
                barrier, device_id=(group, lax.rem(tile + r, TILES)), device_id_type=MESH
            )
        for r in range(1, NY):
            pl.semaphore_signal(barrier, device_id=(in_y(r), tile), device_id_type=MESH)
        for r in range(1, nz):
            pl.semaphore_signal(barrier, device_id=(in_z(r), tile), device_id_type=MESH)

    row_ends, col_ends = [], []
    row_sizes, col_sizes = [], []
    for k in range(pair_count):
        row_sizes.append(rs_ref[k])
        col_sizes.append(cs_ref[k])
        row_ends.append(row_sizes[k] + (row_ends[-1] if k else 0))
        col_ends.append(col_sizes[k] + (col_ends[-1] if k else 0))

    lane = lax.broadcasted_iota(jnp.int32, (LANES, LANES), 1)
    line = lax.broadcasted_iota(jnp.int32, (LANES, LANES), 0)
    eye = lane == line

    def flat(tall):
        return jnp.sum(jnp.where(eye, tall, 0.0), axis=0, keepdims=True)

    def tall(flat_row):
        spread = jnp.where(eye, jnp.broadcast_to(flat_row, (LANES, LANES)), 0.0)
        return jnp.broadcast_to(jnp.sum(spread, axis=1, keepdims=True), (LANES, LANES))

    def squares(block):
        wide = block.astype(jnp.float32)
        total = jnp.sum(wide * wide, axis=1, keepdims=True)
        return jnp.broadcast_to(total, (LANES, LANES))

    with jax.named_scope("column_norms"):

        def column_block(q, carry):
            span = pl.ds(pl.multiple_of(q * LANES, LANES), LANES)
            norm = squares(y_ref[span, :])
            v_wide[span, :] = -shift * norm
            cn[pl.ds(q, 1), :] = flat(norm)
            pair_wide[span, :] = pair_of(tile * n_col + q * LANES + line, col_ends)
            return carry

        lax.fori_loop(0, col_blocks, column_block, 0)

    with jax.named_scope("greeted"):
        pl.semaphore_wait(barrier, TILES - 1 + NY - 1 + nz - 1)
        own_copy.wait()

    def send_block(block, part, to, sem):
        ref = rows.at[block, pl.ds(part * half, half)]
        copy = pltpu.make_async_remote_copy(
            src_ref=ref,
            dst_ref=ref,
            send_sem=send_sem.at[0],
            recv_sem=block_sem.at[sem, part],
            device_id=(group, to),
            device_id_type=MESH,
        )
        copy.start()

    def wait_half(sem, part):
        ref = rows.at[0, pl.ds(0, half)]
        pltpu.make_async_copy(ref, ref, block_sem.at[sem, part]).wait()

    SIB, LEFT, RIGHT, LEFT_SIB, RIGHT_SIB, OPP, OPP_SIB = range(7)
    right, left, sib = at(1, False), at(NX - 1, False), at(0, True)

    with jax.named_scope("send_own"):
        send_block(tile, 0, right, LEFT)
        send_block(tile, 1, left, RIGHT)
        send_block(tile, 1, right, LEFT)
        send_block(tile, 0, left, RIGHT)
        send_block(tile, 0, sib, SIB)
        send_block(tile, 1, sib, SIB)

    row_box[0, tile] = jnp.zeros(row_box.shape[2:], jnp.float32)
    for h in range(2):
        row_box[0, tile, pl.ds(halves + h, 1), :] = flat(
            squares(rows[tile, pl.ds(h * half, half), :])
        )

    chunk = min(512, n_col)

    def score_block(block):
        first = group * (n_row * TILES) + block * n_row
        block_pair = [
            pair_of(first + h * half + lane[:1], row_ends) for h in range(2)
        ]

        def product(i, top):
            span = pl.ds(pl.multiple_of(i * chunk, chunk), chunk)
            cross = lax.dot_general(
                y_ref[span, :],
                rows[block],
                (((1,), (1,)), ((), ())),
                preferred_element_type=jnp.float32,
            )
            v = v_wide[span, :]
            col_pair = pair_wide[span, :]
            new = []
            for h in range(2):
                k = jnp.where(
                    col_pair == block_pair[h], cross[:, h * half : (h + 1) * half] * scale, NEG
                )
                scores[2 * block + h, span, :] = k
                new.append(
                    jnp.maximum(top[h], jnp.max((k + v).reshape(chunk // 8, 8, LANES), axis=0))
                )
            return tuple(new)

        start = jnp.full((8, LANES), 4 * NEG, jnp.float32)
        top = lax.fori_loop(0, n_col // chunk, product, (start, start))
        top = [jnp.max(t, axis=0, keepdims=True) for t in top]

        def total(i, so_far):
            span = pl.ds(pl.multiple_of(i * LANES, LANES), LANES)
            v = v_wide[span, :]
            new = []
            for h in range(2):
                e = jnp.exp2(scores[2 * block + h, span, :] + v - top[h])
                new.append(so_far[h] + jnp.sum(e.reshape(LANES // 8, 8, LANES), axis=0))
            return tuple(new)

        start = jnp.zeros((8, LANES), jnp.float32)
        sums = lax.fori_loop(0, n_col // LANES, total, (start, start))
        for h in range(2):
            row_box[0, tile, pl.ds(2 * block + h, 1), :] = top[h] + jnp.log2(
                jnp.sum(sums[h], axis=0, keepdims=True)
            )

    def score_blocks(dx, flip):
        score_block(at(dx, flip))

    with jax.named_scope("scores_near"):
        score_blocks(0, False)
        wait_half(SIB, 0)
        wait_half(SIB, 1)
        score_blocks(0, True)

    left_block, right_block = at(NX - 1, False), at(1, False)
    opposite = at(2, False)
    with jax.named_scope("forward"):
        wait_half(LEFT, 0)
        send_block(left_block, 0, right, OPP)
        send_block(left_block, 0, sib, LEFT_SIB)
        wait_half(RIGHT, 1)
        send_block(right_block, 1, left, OPP)
        send_block(right_block, 1, sib, RIGHT_SIB)
        wait_half(LEFT, 1)
        send_block(left_block, 1, sib, LEFT_SIB)
        wait_half(RIGHT, 0)
        send_block(right_block, 0, sib, RIGHT_SIB)

    with jax.named_scope("scores_sides"):

        def side(s, carry):
            score_block(2 * lax.rem(x + 1 + 2 * s, NX) + core)
            return carry

        lax.fori_loop(0, 2, side, 0)
        for part in range(2):
            wait_half(LEFT_SIB, part)
            wait_half(RIGHT_SIB, part)

        def other_side(s, carry):
            score_block(2 * lax.rem(x + 1 + 2 * s, NX) + 1 - core)
            return carry

        lax.fori_loop(0, 2, other_side, 0)

    with jax.named_scope("wait_opposite"):
        for part in range(2):
            wait_half(OPP, part)
            send_block(opposite, part, sib, OPP_SIB)
    with jax.named_scope("scores_opposite"):
        score_blocks(2, False)
        for part in range(2):
            wait_half(OPP_SIB, part)
        score_blocks(2, True)

    row_line = lax.broadcasted_iota(jnp.int32, (halves, LANES), 0)
    row_lane = lax.broadcasted_iota(jnp.int32, (halves, LANES), 1)
    row_pair = pair_of(group * (n_row * TILES) + row_line * half + row_lane, row_ends)
    log_cs = jnp.log2(size_of(row_pair, col_sizes))
    col_line = lax.broadcasted_iota(jnp.int32, (col_blocks, LANES), 0)
    col_lane = lax.broadcasted_iota(jnp.int32, (col_blocks, LANES), 1)
    col_pair = pair_of(tile * n_col + col_line * LANES + col_lane, col_ends)
    log_rs = jnp.log2(size_of(col_pair, row_sizes))

    def row_pass(step):
        def highest(i, top):
            span = pl.ds(pl.multiple_of(i * 8, 8), 8)
            return jnp.maximum(top, scores[:, span, :] + v_wide[span, :][None])

        start = jnp.full((halves, 8, LANES), 4 * NEG, jnp.float32)
        top = lax.fori_loop(0, n_col // 8, highest, start, unroll=4)
        top = jnp.max(top, axis=1)

        def total(i, so_far):
            span = pl.ds(pl.multiple_of(i * 8, 8), 8)
            return so_far + jnp.exp2(scores[:, span, :] + v_wide[span, :][None] - top[:, None, :])

        start = jnp.zeros((halves, 8, LANES), jnp.float32)
        sums = lax.fori_loop(0, n_col // 8, total, start, unroll=4)
        row_box[step, tile, :halves, :] = top + jnp.log2(jnp.sum(sums, axis=1))

    def column_pass(u):
        u_wide = u[:, None, :]

        def highest(i, carry):
            span = pl.ds(pl.multiple_of(i * 8, 8), 8)
            top = jnp.max(scores[:, span, :] + u_wide, axis=0)
            top_wide[span, :] = jnp.broadcast_to(jnp.max(top, axis=1, keepdims=True), (8, LANES))
            return carry

        lax.fori_loop(0, n_col // 8, highest, 0, unroll=4)

        def total(i, carry):
            span = pl.ds(pl.multiple_of(i * 8, 8), 8)
            top = top_wide[span, :]
            e = jnp.sum(jnp.exp2(scores[:, span, :] + u_wide - top[None]), axis=0)
            lse = top + jnp.log2(jnp.sum(e, axis=1, keepdims=True))
            top_wide[span, :] = jnp.broadcast_to(lse, (8, LANES))
            return carry

        lax.fori_loop(0, n_col // 8, total, 0, unroll=4)
        for q in range(col_blocks):
            column[pl.ds(q, 1), :] = flat(top_wide[pl.ds(q * LANES, LANES), :])
        return column[...]

    def share(box, step, me, size, targets, send, recv):
        slot = box.at[step, me, pl.ds(0, size)]
        for to in targets:
            pltpu.make_async_remote_copy(
                src_ref=slot,
                dst_ref=slot,
                send_sem=send,
                recv_sem=recv,
                device_id=to,
                device_id_type=MESH,
            ).start()
        some = box.at[step, pl.ds(0, len(targets)), pl.ds(0, size)]
        pltpu.make_async_copy(some, some, recv).wait()

    def sent(box, step, count, size, send):
        some = box.at[step, pl.ds(0, count), pl.ds(0, size)]
        pltpu.make_async_copy(some, some, send).wait()

    z_targets = []
    for step in range(ITERS):
        last = step + 1 == ITERS
        if step:
            with jax.named_scope("row_pass"):
                row_pass(step)
        with jax.named_scope("row_share"):
            share(
                row_box,
                step,
                tile,
                row_box.shape[2] if step == 0 else halves,
                [(group, lax.rem(tile + r, TILES)) for r in range(1, TILES)],
                send_sem.at[1 + 3 * step],
                row_sem.at[step],
            )
            u = log_cs - merged(row_box[step, :, :halves, :])
        with jax.named_scope("column_pass"):
            y_box[step, y, :col_blocks, :] = column_pass(u)
        size = col_blocks
        if last:
            size = col_blocks + pair_count
            f = (EPS / LOG2E) * u
            f = f + jnp.concatenate(
                [row_box[0, t, halves : halves + 2, :] for t in range(TILES)], axis=0
            ) * (1.0 / depth)
            for k in range(pair_count):
                y_box[step, y, pl.ds(col_blocks + k, 1), :] = jnp.sum(
                    jnp.where(row_pair == k, f, 0.0), axis=0, keepdims=True
                )
        with jax.named_scope("column_share_y"):
            share(
                y_box,
                step,
                y,
                size,
                [(in_y(r), tile) for r in range(1, NY)],
                send_sem.at[2 + 3 * step],
                y_sem.at[step],
            )
            lse = merged(y_box[step, :, :col_blocks, :])
            z_box[step, z, :col_blocks, :] = lse
            if last:
                z_box[step, z, col_blocks:, :] = jnp.sum(y_box[step, :, col_blocks:, :], axis=0)
        with jax.named_scope("column_share_z"):
            if last:
                near = list(range(1, nz))
            else:
                near = sorted({r % nz for r in range(-window, window + 1)} - {0})
            z_targets.append(len(near))
            if len(near) < nz - 1:
                for r in range(1, nz):
                    if r not in near:
                        z_box[step, lax.rem(z + r, nz), :col_blocks, :] = jnp.full(
                            (col_blocks, LANES), NEG, jnp.float32
                        )
            share(
                z_box,
                step,
                z,
                size,
                [(in_z(r), tile) for r in near],
                send_sem.at[3 + 3 * step],
                z_sem.at[step],
            )
            lse = merged(z_box[step, :, :col_blocks, :])
            v = jnp.where(lse > EMPTY, log_rs - lse, 0.0)
        if not last:
            with jax.named_scope("spread"):
                for q in range(col_blocks):
                    v_wide[pl.ds(q * LANES, LANES), :] = tall(v[q : q + 1, :])

    with jax.named_scope("results"):
        g_ref[...] = (EPS / LOG2E) * v + cn[...] * (1.0 / depth)
        sums = jnp.sum(z_box[ITERS - 1, :, col_blocks:, :], axis=0)
        sums = jnp.broadcast_to(jnp.sum(sums, axis=1, keepdims=True), (pair_count, LANES))
        value = jnp.zeros((2, LANES), jnp.float32)
        own_pair = jnp.zeros((2, LANES), jnp.int32)
        for t in range(TILES):
            value = jnp.where(tile == t, f[2 * t : 2 * t + 2], value)
            own_pair = jnp.where(tile == t, row_pair[2 * t : 2 * t + 2], own_pair)
        mean = jnp.zeros((2, LANES), jnp.float32)
        for k in range(pair_count):
            mean = jnp.where(own_pair == k, sums[k : k + 1, :], mean)
        f_ref[...] = value - mean / size_of(own_pair, row_sizes)

    with jax.named_scope("sent"):
        ref = rows.at[pl.ds(0, 7)]
        pltpu.make_async_copy(ref, ref, send_sem.at[0]).wait()
        for step in range(ITERS):
            last = step + 1 == ITERS
            width = row_box.shape[2] if step == 0 else halves
            size = col_blocks + (pair_count if last else 0)
            sent(row_box, step, TILES - 1, width, send_sem.at[1 + 3 * step])
            sent(y_box, step, NY - 1, size, send_sem.at[2 + 3 * step])
            sent(z_box, step, z_targets[step], size, send_sem.at[3 + 3 * step])


def local(candidates, validation, row_sizes, col_sizes):
    groups = lax.axis_size("pair")
    n_row, depth = candidates.shape
    n_col = validation.shape[0]
    pairs = row_sizes.shape[0]
    halves = 2 * TILES
    half = n_row // 2
    col_blocks = n_col // LANES
    vmem = pl.BlockSpec(memory_space=pltpu.VMEM)
    smem = pl.BlockSpec(memory_space=pltpu.SMEM)
    row_value, col_potential = pl.pallas_call(
        functools.partial(kernel, pairs, groups),
        out_shape=(
            jax.ShapeDtypeStruct((2, half), jnp.float32),
            jax.ShapeDtypeStruct((col_blocks, LANES), jnp.float32),
        ),
        in_specs=[smem, smem, vmem, vmem],
        out_specs=(vmem, vmem),
        scratch_shapes=[
            pltpu.VMEM((TILES, n_row, depth), jnp.bfloat16),
            pltpu.VMEM((halves, n_col, half), jnp.float32),
            pltpu.VMEM((n_col, LANES), jnp.float32),
            pltpu.VMEM((n_col, LANES), jnp.int32),
            pltpu.VMEM((n_col, LANES), jnp.float32),
            pltpu.VMEM((col_blocks, LANES), jnp.float32),
            pltpu.VMEM((col_blocks, LANES), jnp.float32),
            pltpu.VMEM((ITERS, TILES, halves + 8, half), jnp.float32),
            pltpu.VMEM((ITERS, NY, col_blocks + pairs, LANES), jnp.float32),
            pltpu.VMEM((ITERS, groups // NY, col_blocks + pairs, LANES), jnp.float32),
            pltpu.SemaphoreType.DMA,
            pltpu.SemaphoreType.DMA((1 + 3 * ITERS,)),
            pltpu.SemaphoreType.DMA((7, 2)),
            pltpu.SemaphoreType.DMA((ITERS,)),
            pltpu.SemaphoreType.DMA((ITERS,)),
            pltpu.SemaphoreType.DMA((ITERS,)),
        ],
        compiler_params=pltpu.CompilerParams(
            collective_id=0, has_side_effects=True, vmem_limit_bytes=48 * 2**20
        ),
    )(row_sizes, col_sizes, candidates, validation)
    return row_value.reshape(n_row), col_potential.reshape(n_col)


def solution(mesh):
    in_specs = (P(("pair", "tile"), None), P("tile", None), P(), P())
    out_specs = (P(("pair", "tile")), P("tile"))
    return jax.shard_map(local, mesh=mesh, in_specs=in_specs, out_specs=out_specs, check_vma=False)
```

time: 836 us -> 113 us (0.14)
  the two profiles are of different devices: /device:TPU:2 before, /device:TPU:1 now
where the time goes in v1:
time: 113 us; the launch traced here: 111 us
  Pallas kernels  105 us (93%)
  local copies, waits for them, and re-layouts  4.86 us (4%)
    pallas_call x1, Pallas kernels, local(): pl.pallas_call(functools.partial(kernel, pairs, groups), out_shape=(jax.S...  105 us
    unnamed x10, local copies, waits for them, and re-layouts  4.86 us

profile of v1, /device:TPU:1, one launch (start us, length us, event | category | flops | bytes accessed | tf_op | source)
XLA Modules:
  0.0 110.7 jit_solution(4038859321129443342)
XLA Ops:
  0.6 0.0 copy-start
  0.6 1.4 %copy-done = bf16[1024,768]{1,0:T(8,128)(2,1)S(1)} copy-done((bf16[1024,768]{1,0:T(8,128)(2,1)S(1)}, bf16[1024,768]{1,0:T(8,128)(2,1)}, u32[]{:S(2)}) %copy-start) | copy-done | bytes 1572888
  2.0 0.0 copy-start.1
  2.0 1.0 copy-done.1
  3.0 0.0 copy-start.2
  3.0 0.7 copy-done.2
  3.7 0.0 copy-start.3
  3.7 0.7 copy-done.3
  4.3 105.2 %shard_map.59 = (f32[2,128]{1,0:T(2,128)S(1)}, f32[8,128]{1,0:T(8,128)S(1)}) custom-call(s32[16]{0:T(128)S(1)} %copy-done.2, s32[16]{0:T(128)S(1)} %copy-done.3, bf16[256,768]{1,0:T(8,128)(2,1)S(1)} %copy-done.1, bf16[1024,768]{1,0:T(8,128)(2,1)S(1)} %copy-done), custom_call_target="tpu_custom_call" | custom-call | tf_op jit(solution)/shard_map/pallas_call | solution.py:454
  109.5 0.6 copy.8
  110.1 0.6 copy.9
Async XLA Ops:
  0.6 1.4 %copy-start = (bf16[1024,768]{1,0:T(8,128)(2,1)S(1)}, bf16[1024,768]{1,0:T(8,128)(2,1)}, u32[]{:S(2)}) copy-start(bf16[1024,768]{1,0:T(8,128)(2,1)} %y_ref.1) | copy-start | bytes 4718596
  2.0 1.0 copy-start.1
  3.0 0.7 copy-start.2
  3.7 0.7 copy-start.3

commit v2 on v1

--- a/solution.py
+++ b/solution.py
@@ -42,26 +42,32 @@
 def kernel(
     pair_count,
     group_count,
+    rs_hbm,
+    cs_hbm,
+    x_ref,
+    y_hbm,
+    f_ref,
+    g_ref,
     rs_ref,
     cs_ref,
-    x_ref,
     y_ref,
-    f_ref,
-    g_ref,
     rows,
     scores,
     v_wide,
     pair_wide,
     top_wide,
+    sum_wide,
     cn,
     column,
     row_box,
+    near_box,
     y_box,
     z_box,
     local_sem,
     send_sem,
     block_sem,
     row_sem,
+    near_sem,
     y_sem,
     z_sem,
 ):
@@ -71,7 +77,7 @@
     halves = 2 * TILES
     col_blocks = n_col // LANES
     nz = group_count // NY
-    window = min(-(-ROW_MOST // (n_row * TILES * NY)), nz // 2)
+    reach = -(-ROW_MOST // (n_row * TILES))
     scale = 2.0 * LOG2E / (depth * EPS)
     shift = LOG2E / (depth * EPS)
 
@@ -91,57 +97,24 @@
         return lax.rem(z + r, nz) * NY + y
 
     with jax.named_scope("greet"):
-        own_copy = pltpu.make_async_copy(x_ref, rows.at[tile], local_sem)
-        own_copy.start()
+        near = [(lax.rem(group + r + group_count, group_count), tile) for r in range(-reach, reach + 1) if r]
+        copies = [
+            pltpu.make_async_copy(a, b, local_sem.at[i])
+            for i, (a, b) in enumerate(
+                [(x_ref, rows.at[tile]), (rs_hbm, rs_ref), (cs_hbm, cs_ref), (y_hbm, y_ref)]
+            )
+        ]
+        for copy in copies:
+            copy.start()
         barrier = pltpu.get_barrier_semaphore()
         for r in range(1, TILES):
             pl.semaphore_signal(
                 barrier, device_id=(group, lax.rem(tile + r, TILES)), device_id_type=MESH
             )
-        for r in range(1, NY):
-            pl.semaphore_signal(barrier, device_id=(in_y(r), tile), device_id_type=MESH)
-        for r in range(1, nz):
-            pl.semaphore_signal(barrier, device_id=(in_z(r), tile), device_id_type=MESH)
-
-    row_ends, col_ends = [], []
-    row_sizes, col_sizes = [], []
-    for k in range(pair_count):
-        row_sizes.append(rs_ref[k])
-        col_sizes.append(cs_ref[k])
-        row_ends.append(row_sizes[k] + (row_ends[-1] if k else 0))
-        col_ends.append(col_sizes[k] + (col_ends[-1] if k else 0))
-
-    lane = lax.broadcasted_iota(jnp.int32, (LANES, LANES), 1)
-    line = lax.broadcasted_iota(jnp.int32, (LANES, LANES), 0)
-    eye = lane == line
-
-    def flat(tall):
-        return jnp.sum(jnp.where(eye, tall, 0.0), axis=0, keepdims=True)
-
-    def tall(flat_row):
-        spread = jnp.where(eye, jnp.broadcast_to(flat_row, (LANES, LANES)), 0.0)
-        return jnp.broadcast_to(jnp.sum(spread, axis=1, keepdims=True), (LANES, LANES))
-
-    def squares(block):
-        wide = block.astype(jnp.float32)
-        total = jnp.sum(wide * wide, axis=1, keepdims=True)
-        return jnp.broadcast_to(total, (LANES, LANES))
-
-    with jax.named_scope("column_norms"):
-
-        def column_block(q, carry):
-            span = pl.ds(pl.multiple_of(q * LANES, LANES), LANES)
-            norm = squares(y_ref[span, :])
-            v_wide[span, :] = -shift * norm
-            cn[pl.ds(q, 1), :] = flat(norm)
-            pair_wide[span, :] = pair_of(tile * n_col + q * LANES + line, col_ends)
-            return carry
-
-        lax.fori_loop(0, col_blocks, column_block, 0)
-
-    with jax.named_scope("greeted"):
-        pl.semaphore_wait(barrier, TILES - 1 + NY - 1 + nz - 1)
-        own_copy.wait()
+        for to in near:
+            pl.semaphore_signal(barrier, device_id=to, device_id_type=MESH)
+        copies[0].wait()
+        pl.semaphore_wait(barrier, TILES - 1 + len(near))
 
     def send_block(block, part, to, sem):
         ref = rows.at[block, pl.ds(part * half, half)]
@@ -169,6 +142,46 @@
         send_block(tile, 0, left, RIGHT)
         send_block(tile, 0, sib, SIB)
         send_block(tile, 1, sib, SIB)
+
+    with jax.named_scope("inputs"):
+        for copy in copies[1:]:
+            copy.wait()
+
+    row_ends, col_ends = [], []
+    row_sizes, col_sizes = [], []
+    for k in range(pair_count):
+        row_sizes.append(rs_ref[k])
+        col_sizes.append(cs_ref[k])
+        row_ends.append(row_sizes[k] + (row_ends[-1] if k else 0))
+        col_ends.append(col_sizes[k] + (col_ends[-1] if k else 0))
+
+    lane = lax.broadcasted_iota(jnp.int32, (LANES, LANES), 1)
+    line = lax.broadcasted_iota(jnp.int32, (LANES, LANES), 0)
+    eye = lane == line
+
+    def flat(tall):
+        return jnp.sum(jnp.where(eye, tall, 0.0), axis=0, keepdims=True)
+
+    def tall(flat_row):
+        spread = jnp.where(eye, jnp.broadcast_to(flat_row, (LANES, LANES)), 0.0)
+        return jnp.broadcast_to(jnp.sum(spread, axis=1, keepdims=True), (LANES, LANES))
+
+    def squares(block):
+        wide = block.astype(jnp.float32)
+        total = jnp.sum(wide * wide, axis=1, keepdims=True)
+        return jnp.broadcast_to(total, (LANES, LANES))
+
+    with jax.named_scope("column_norms"):
+
+        def column_block(q, carry):
+            span = pl.ds(pl.multiple_of(q * LANES, LANES), LANES)
+            norm = squares(y_ref[span, :])
+            v_wide[span, :] = -shift * norm
+            cn[pl.ds(q, 1), :] = flat(norm)
+            pair_wide[span, :] = pair_of(tile * n_col + q * LANES + line, col_ends)
+            return carry
+
+        lax.fori_loop(0, col_blocks, column_block, 0)
 
     row_box[0, tile] = jnp.zeros(row_box.shape[2:], jnp.float32)
     for h in range(2):
@@ -302,35 +315,38 @@
         row_box[step, tile, :halves, :] = top + jnp.log2(jnp.sum(sums, axis=1))
 
     def column_pass(u):
-        u_wide = u[:, None, :]
-
-        def highest(i, carry):
+        u_wide = jnp.broadcast_to(u[:, None, :], (halves, 8, LANES))
+
+        def lanes(i, carry):
             span = pl.ds(pl.multiple_of(i * 8, 8), 8)
-            top = jnp.max(scores[:, span, :] + u_wide, axis=0)
-            top_wide[span, :] = jnp.broadcast_to(jnp.max(top, axis=1, keepdims=True), (8, LANES))
+            t = scores[:, span, :] + u_wide
+            top = jnp.max(t, axis=0)
+            top_wide[span, :] = top
+            sum_wide[span, :] = jnp.sum(jnp.exp2(t - top[None]), axis=0)
             return carry
 
-        lax.fori_loop(0, n_col // 8, highest, 0, unroll=4)
-
-        def total(i, carry):
-            span = pl.ds(pl.multiple_of(i * 8, 8), 8)
-            top = top_wide[span, :]
-            e = jnp.sum(jnp.exp2(scores[:, span, :] + u_wide - top[None]), axis=0)
-            lse = top + jnp.log2(jnp.sum(e, axis=1, keepdims=True))
-            top_wide[span, :] = jnp.broadcast_to(lse, (8, LANES))
+        lax.fori_loop(0, n_col // 8, lanes, 0, unroll=2)
+
+        def across(q, carry):
+            span = pl.ds(pl.multiple_of(q * LANES, LANES), LANES)
+            tops = top_wide[span, :]
+            top = jnp.max(tops, axis=1, keepdims=True)
+            total = jnp.sum(sum_wide[span, :] * jnp.exp2(tops - top), axis=1, keepdims=True)
+            wide = (LANES, LANES)
+            column[pl.ds(q, 1), :] = flat(jnp.broadcast_to(top, wide)) + jnp.log2(
+                flat(jnp.broadcast_to(total, wide))
+            )
             return carry
 
-        lax.fori_loop(0, n_col // 8, total, 0, unroll=4)
-        for q in range(col_blocks):
-            column[pl.ds(q, 1), :] = flat(top_wide[pl.ds(q * LANES, LANES), :])
+        lax.fori_loop(0, col_blocks, across, 0, unroll=2)
         return column[...]
 
     def share(box, step, me, size, targets, send, recv):
-        slot = box.at[step, me, pl.ds(0, size)]
-        for to in targets:
+        own = box.at[step, len(targets) if me is None else me, pl.ds(0, size)]
+        for i, to in enumerate(targets):
             pltpu.make_async_remote_copy(
-                src_ref=slot,
-                dst_ref=slot,
+                src_ref=own,
+                dst_ref=box.at[step, i, pl.ds(0, size)] if me is None else own,
                 send_sem=send,
                 recv_sem=recv,
                 device_id=to,
@@ -343,7 +359,6 @@
         some = box.at[step, pl.ds(0, count), pl.ds(0, size)]
         pltpu.make_async_copy(some, some, send).wait()
 
-    z_targets = []
     for step in range(ITERS):
         last = step + 1 == ITERS
         if step:
@@ -356,60 +371,60 @@
                 tile,
                 row_box.shape[2] if step == 0 else halves,
                 [(group, lax.rem(tile + r, TILES)) for r in range(1, TILES)],
-                send_sem.at[1 + 3 * step],
+                send_sem.at[1 + step],
                 row_sem.at[step],
             )
             u = log_cs - merged(row_box[step, :, :halves, :])
         with jax.named_scope("column_pass"):
-            y_box[step, y, :col_blocks, :] = column_pass(u)
-        size = col_blocks
-        if last:
-            size = col_blocks + pair_count
+            column_lse = column_pass(u)
+        if not last:
+            with jax.named_scope("column_share_near"):
+                near_box[step, len(near)] = column_lse
+                share(
+                    near_box,
+                    step,
+                    None,
+                    col_blocks,
+                    near,
+                    send_sem.at[1 + ITERS + step],
+                    near_sem.at[step],
+                )
+                lse = merged(near_box[step])
+                v = jnp.where(lse > EMPTY, log_rs - lse, 0.0)
+        else:
             f = (EPS / LOG2E) * u
             f = f + jnp.concatenate(
                 [row_box[0, t, halves : halves + 2, :] for t in range(TILES)], axis=0
             ) * (1.0 / depth)
+            size = col_blocks + pair_count
+            y_box[0, y, :col_blocks, :] = column_lse
             for k in range(pair_count):
-                y_box[step, y, pl.ds(col_blocks + k, 1), :] = jnp.sum(
+                y_box[0, y, pl.ds(col_blocks + k, 1), :] = jnp.sum(
                     jnp.where(row_pair == k, f, 0.0), axis=0, keepdims=True
                 )
-        with jax.named_scope("column_share_y"):
-            share(
-                y_box,
-                step,
-                y,
-                size,
-                [(in_y(r), tile) for r in range(1, NY)],
-                send_sem.at[2 + 3 * step],
-                y_sem.at[step],
-            )
-            lse = merged(y_box[step, :, :col_blocks, :])
-            z_box[step, z, :col_blocks, :] = lse
-            if last:
-                z_box[step, z, col_blocks:, :] = jnp.sum(y_box[step, :, col_blocks:, :], axis=0)
-        with jax.named_scope("column_share_z"):
-            if last:
-                near = list(range(1, nz))
-            else:
-                near = sorted({r % nz for r in range(-window, window + 1)} - {0})
-            z_targets.append(len(near))
-            if len(near) < nz - 1:
-                for r in range(1, nz):
-                    if r not in near:
-                        z_box[step, lax.rem(z + r, nz), :col_blocks, :] = jnp.full(
-                            (col_blocks, LANES), NEG, jnp.float32
-                        )
-            share(
-                z_box,
-                step,
-                z,
-                size,
-                [(in_z(r), tile) for r in near],
-                send_sem.at[3 + 3 * step],
-                z_sem.at[step],
-            )
-            lse = merged(z_box[step, :, :col_blocks, :])
-            v = jnp.where(lse > EMPTY, log_rs - lse, 0.0)
+            with jax.named_scope("column_share_y"):
+                share(
+                    y_box,
+                    0,
+                    y,
+                    size,
+                    [(in_y(r), tile) for r in range(1, NY)],
+                    send_sem.at[2 * ITERS],
+                    y_sem,
+                )
+                z_box[0, z, :col_blocks, :] = merged(y_box[0, :, :col_blocks, :])
+                z_box[0, z, col_blocks:, :] = jnp.sum(y_box[0, :, col_blocks:, :], axis=0)
+            with jax.named_scope("column_share_z"):
+                share(
+                    z_box,
+                    0,
+                    z,
+                    size,
+                    [(in_z(r), tile) for r in range(1, nz)],
+                    send_sem.at[2 * ITERS + 1],
+                    z_sem,
+                )
+                v = log_rs - merged(z_box[0, :, :col_blocks, :])
         if not last:
             with jax.named_scope("spread"):
                 for q in range(col_blocks):
@@ -417,7 +432,7 @@
 
     with jax.named_scope("results"):
         g_ref[...] = (EPS / LOG2E) * v + cn[...] * (1.0 / depth)
-        sums = jnp.sum(z_box[ITERS - 1, :, col_blocks:, :], axis=0)
+        sums = jnp.sum(z_box[0, :, col_blocks:, :], axis=0)
         sums = jnp.broadcast_to(jnp.sum(sums, axis=1, keepdims=True), (pair_count, LANES))
         value = jnp.zeros((2, LANES), jnp.float32)
         own_pair = jnp.zeros((2, LANES), jnp.int32)
@@ -433,12 +448,12 @@
         ref = rows.at[pl.ds(0, 7)]
         pltpu.make_async_copy(ref, ref, send_sem.at[0]).wait()
         for step in range(ITERS):
-            last = step + 1 == ITERS
             width = row_box.shape[2] if step == 0 else halves
-            size = col_blocks + (pair_count if last else 0)
-            sent(row_box, step, TILES - 1, width, send_sem.at[1 + 3 * step])
-            sent(y_box, step, NY - 1, size, send_sem.at[2 + 3 * step])
-            sent(z_box, step, z_targets[step], size, send_sem.at[3 + 3 * step])
+            sent(row_box, step, TILES - 1, width, send_sem.at[1 + step])
+        for step in range(ITERS - 1):
+            sent(near_box, step, len(near), col_blocks, send_sem.at[1 + ITERS + step])
+        sent(y_box, 0, NY - 1, size, send_sem.at[2 * ITERS])
+        sent(z_box, 0, nz - 1, size, send_sem.at[2 * ITERS + 1])
 
 
 def local(candidates, validation, row_sizes, col_sizes):
@@ -450,35 +465,42 @@
     half = n_row // 2
     col_blocks = n_col // LANES
     vmem = pl.BlockSpec(memory_space=pltpu.VMEM)
-    smem = pl.BlockSpec(memory_space=pltpu.SMEM)
+    whole = pl.BlockSpec(memory_space=pl.ANY)
+    near = 2 * -(-ROW_MOST // (n_row * TILES))
     row_value, col_potential = pl.pallas_call(
         functools.partial(kernel, pairs, groups),
         out_shape=(
             jax.ShapeDtypeStruct((2, half), jnp.float32),
             jax.ShapeDtypeStruct((col_blocks, LANES), jnp.float32),
         ),
-        in_specs=[smem, smem, vmem, vmem],
+        in_specs=[whole] * 4,
         out_specs=(vmem, vmem),
         scratch_shapes=[
+            pltpu.SMEM((pairs,), jnp.int32),
+            pltpu.SMEM((pairs,), jnp.int32),
+            pltpu.VMEM((n_col, depth), jnp.bfloat16),
             pltpu.VMEM((TILES, n_row, depth), jnp.bfloat16),
             pltpu.VMEM((halves, n_col, half), jnp.float32),
             pltpu.VMEM((n_col, LANES), jnp.float32),
             pltpu.VMEM((n_col, LANES), jnp.int32),
             pltpu.VMEM((n_col, LANES), jnp.float32),
+            pltpu.VMEM((n_col, LANES), jnp.float32),
             pltpu.VMEM((col_blocks, LANES), jnp.float32),
             pltpu.VMEM((col_blocks, LANES), jnp.float32),
             pltpu.VMEM((ITERS, TILES, halves + 8, half), jnp.float32),
-            pltpu.VMEM((ITERS, NY, col_blocks + pairs, LANES), jnp.float32),
-            pltpu.VMEM((ITERS, groups // NY, col_blocks + pairs, LANES), jnp.float32),
-            pltpu.SemaphoreType.DMA,
-            pltpu.SemaphoreType.DMA((1 + 3 * ITERS,)),
+            pltpu.VMEM((ITERS - 1, near + 1, col_blocks, LANES), jnp.float32),
+            pltpu.VMEM((1, NY, col_blocks + pairs, LANES), jnp.float32),
+            pltpu.VMEM((1, groups // NY, col_blocks + pairs, LANES), jnp.float32),
+            pltpu.SemaphoreType.DMA((4,)),
+            pltpu.SemaphoreType.DMA((2 * ITERS + 2,)),
             pltpu.SemaphoreType.DMA((7, 2)),
             pltpu.SemaphoreType.DMA((ITERS,)),
-            pltpu.SemaphoreType.DMA((ITERS,)),
-            pltpu.SemaphoreType.DMA((ITERS,)),
+            pltpu.SemaphoreType.DMA((ITERS - 1,)),
+            pltpu.SemaphoreType.DMA,
+            pltpu.SemaphoreType.DMA,
         ],
         compiler_params=pltpu.CompilerParams(
-            collective_id=0, has_side_effects=True, vmem_limit_bytes=48 * 2**20
+            collective_id=0, has_side_effects=True, vmem_limit_bytes=56 * 2**20
         ),
     )(row_sizes, col_sizes, candidates, validation)
     return row_value.reshape(n_row), col_potential.reshape(n_col)

time: 113 us -> 91.4 us (0.81); the launches traced: 111 us -> 91.2 us
  Pallas kernels: 105 us -> 88.1 us
  local copies, waits for them, and re-layouts: 4.86 us -> 2.48 us
    pallas_call x1, Pallas kernels: 105 us -> 88.1 us  [local(): pl.pallas_call(functools.partial(kernel, pairs, groups), out_shape=(jax.S...]
    unnamed x10 -> x2, local copies, waits for them, and re-layouts: 4.86 us -> 2.48 us
where the time goes in v2:
time: 91.4 us; the launch traced here: 91.2 us
  Pallas kernels  88.1 us (96%)
  local copies, waits for them, and re-layouts  2.48 us (3%)
    pallas_call x1, Pallas kernels, local(): pl.pallas_call(functools.partial(kernel, pairs, groups), out_shape=(jax.S...  88.1 us
    unnamed x2, local copies, waits for them, and re-layouts  2.48 us

profile of v2, /device:TPU:1, one launch (start us, length us, event | category | flops | bytes accessed | tf_op | source)
XLA Modules:
  0.0 91.2 jit_solution(12273716591657886697)
XLA Ops:
  0.6 88.1 %shard_map.59 = (f32[2,128]{1,0:T(2,128)}, f32[8,128]{1,0:T(8,128)}) custom-call(s32[16]{0:T(128)} %rs_hbm.1, s32[16]{0:T(128)} %cs_hbm.1, bf16[256,768]{1,0:T(8,128)(2,1)} %x_ref.1, bf16[1024,768]{1,0:T(8,128)(2,1)} %y_hbm.1), custom_call_target="tpu_custom_call" | custom-call | tf_op jit(solution)/shard_map/pallas_call | solution.py:470
  88.8 1.2 %copy.8 = f32[256]{0:T(256)} copy(f32[256]{0:T(256)} %bitcast.3) | data formatting | bytes 2048
  90.0 1.3 %copy.9 = f32[1024]{0:T(1024)} copy(f32[1024]{0:T(1024)} %bitcast.2) | data formatting | bytes 8192

commit v3 on v2

--- a/solution.py
+++ b/solution.py
@@ -12,10 +12,12 @@
 EPS = 0.02
 NEG = -1e30
 EMPTY = -1e29
+TINY = 1e-37
 LOG2E = math.log2(math.e)
 NX, NY = 4, 4
 TILES = 2 * NX
 ROW_MOST = 24576
+HOPS = 4
 LANES = 128
 MESH = pl.DeviceIdType.MESH
 
@@ -66,6 +68,7 @@
     local_sem,
     send_sem,
     block_sem,
+    hop_sem,
     row_sem,
     near_sem,
     y_sem,
@@ -98,6 +101,7 @@
 
     with jax.named_scope("greet"):
         near = [(lax.rem(group + r + group_count, group_count), tile) for r in range(-reach, reach + 1) if r]
+        neighbours = [(in_y(1), tile), (in_y(NY - 1), tile), (in_z(1), tile), (in_z(nz - 1), tile)]
         copies = [
             pltpu.make_async_copy(a, b, local_sem.at[i])
             for i, (a, b) in enumerate(
@@ -107,21 +111,24 @@
         for copy in copies:
             copy.start()
         barrier = pltpu.get_barrier_semaphore()
-        for r in range(1, TILES):
-            pl.semaphore_signal(
-                barrier, device_id=(group, lax.rem(tile + r, TILES)), device_id_type=MESH
-            )
-        for to in near:
+        for to in neighbours + [(group, at(dx, flip)) for dx, flip in ((1, 0), (NX - 1, 0), (0, 1))]:
             pl.semaphore_signal(barrier, device_id=to, device_id_type=MESH)
         copies[0].wait()
-        pl.semaphore_wait(barrier, TILES - 1 + len(near))
-
-    def send_block(block, part, to, sem):
+        pl.semaphore_wait(barrier, len(neighbours) + 3)
+
+    def tell(r):
+        for to in neighbours:
+            pl.semaphore_signal(hop_sem.at[r - 1], device_id=to, device_id_type=MESH)
+
+    def told(r):
+        pl.semaphore_wait(hop_sem.at[r - 1], len(neighbours))
+
+    def send_block(block, part, to, sem, sent=0):
         ref = rows.at[block, pl.ds(part * half, half)]
         copy = pltpu.make_async_remote_copy(
             src_ref=ref,
             dst_ref=ref,
-            send_sem=send_sem.at[0],
+            send_sem=send_sem.at[sent],
             recv_sem=block_sem.at[sem, part],
             device_id=(group, to),
             device_id_type=MESH,
@@ -136,12 +143,11 @@
     right, left, sib = at(1, False), at(NX - 1, False), at(0, True)
 
     with jax.named_scope("send_own"):
-        send_block(tile, 0, right, LEFT)
-        send_block(tile, 1, left, RIGHT)
-        send_block(tile, 1, right, LEFT)
-        send_block(tile, 0, left, RIGHT)
+        send_block(tile, 0, right, LEFT, 1)
+        send_block(tile, 1, left, RIGHT, 1)
         send_block(tile, 0, sib, SIB)
         send_block(tile, 1, sib, SIB)
+        tell(1)
 
     with jax.named_scope("inputs"):
         for copy in copies[1:]:
@@ -247,6 +253,13 @@
         wait_half(SIB, 1)
         score_blocks(0, True)
 
+    with jax.named_scope("send_own_rest"):
+        pltpu.make_async_copy(rows.at[0], rows.at[0], send_sem.at[1]).wait()
+        send_block(tile, 1, right, LEFT)
+        send_block(tile, 0, left, RIGHT)
+        told(1)
+        tell(2)
+
     left_block, right_block = at(NX - 1, False), at(1, False)
     opposite = at(2, False)
     with jax.named_scope("forward"):
@@ -260,6 +273,8 @@
         send_block(left_block, 1, sib, LEFT_SIB)
         wait_half(RIGHT, 0)
         send_block(right_block, 0, sib, RIGHT_SIB)
+        told(2)
+        tell(3)
 
     with jax.named_scope("scores_sides"):
 
@@ -277,6 +292,8 @@
             return carry
 
         lax.fori_loop(0, 2, other_side, 0)
+        told(3)
+        tell(4)
 
     with jax.named_scope("wait_opposite"):
         for part in range(2):
@@ -291,41 +308,36 @@
     row_line = lax.broadcasted_iota(jnp.int32, (halves, LANES), 0)
     row_lane = lax.broadcasted_iota(jnp.int32, (halves, LANES), 1)
     row_pair = pair_of(group * (n_row * TILES) + row_line * half + row_lane, row_ends)
-    log_cs = jnp.log2(size_of(row_pair, col_sizes))
+    cs_of_row = size_of(row_pair, col_sizes)
+    log_cs = jnp.log2(cs_of_row)
     col_line = lax.broadcasted_iota(jnp.int32, (col_blocks, LANES), 0)
     col_lane = lax.broadcasted_iota(jnp.int32, (col_blocks, LANES), 1)
     col_pair = pair_of(tile * n_col + col_line * LANES + col_lane, col_ends)
-    log_rs = jnp.log2(size_of(col_pair, row_sizes))
-
-    def row_pass(step):
-        def highest(i, top):
+    rs_of_col = size_of(col_pair, row_sizes)
+    log_rs = jnp.log2(rs_of_col)
+
+    def row_sums():
+        def add(i, so_far):
             span = pl.ds(pl.multiple_of(i * 8, 8), 8)
-            return jnp.maximum(top, scores[:, span, :] + v_wide[span, :][None])
-
-        start = jnp.full((halves, 8, LANES), 4 * NEG, jnp.float32)
-        top = lax.fori_loop(0, n_col // 8, highest, start, unroll=4)
-        top = jnp.max(top, axis=1)
-
-        def total(i, so_far):
-            span = pl.ds(pl.multiple_of(i * 8, 8), 8)
-            return so_far + jnp.exp2(scores[:, span, :] + v_wide[span, :][None] - top[:, None, :])
+            return so_far + scores[:, span, :] * v_wide[span, :][None]
 
         start = jnp.zeros((halves, 8, LANES), jnp.float32)
-        sums = lax.fori_loop(0, n_col // 8, total, start, unroll=4)
-        row_box[step, tile, :halves, :] = top + jnp.log2(jnp.sum(sums, axis=1))
-
-    def column_pass(u):
+        return jnp.sum(lax.fori_loop(0, n_col // 8, add, start, unroll=4), axis=1)
+
+    def first_column_pass(u):
         u_wide = jnp.broadcast_to(u[:, None, :], (halves, 8, LANES))
 
         def lanes(i, carry):
             span = pl.ds(pl.multiple_of(i * 8, 8), 8)
             t = scores[:, span, :] + u_wide
             top = jnp.max(t, axis=0)
+            e = jnp.exp2(t - top[None])
+            scores[:, span, :] = e
             top_wide[span, :] = top
-            sum_wide[span, :] = jnp.sum(jnp.exp2(t - top[None]), axis=0)
-            return carry
-
-        lax.fori_loop(0, n_col // 8, lanes, 0, unroll=2)
+            sum_wide[span, :] = jnp.sum(e, axis=0)
+            return carry
+
+        lax.fori_loop(0, n_col // 8, lanes, 0, unroll=4)
 
         def across(q, carry):
             span = pl.ds(pl.multiple_of(q * LANES, LANES), LANES)
@@ -336,6 +348,25 @@
             column[pl.ds(q, 1), :] = flat(jnp.broadcast_to(top, wide)) + jnp.log2(
                 flat(jnp.broadcast_to(total, wide))
             )
+            return carry
+
+        lax.fori_loop(0, col_blocks, across, 0, unroll=2)
+        return column[...]
+
+    def column_sums(b):
+        b_wide = jnp.broadcast_to(b[:, None, :], (halves, 8, LANES))
+
+        def lanes(i, carry):
+            span = pl.ds(pl.multiple_of(i * 8, 8), 8)
+            sum_wide[span, :] = jnp.sum(scores[:, span, :] * b_wide, axis=0) * top_wide[span, :]
+            return carry
+
+        lax.fori_loop(0, n_col // 8, lanes, 0, unroll=4)
+
+        def across(q, carry):
+            span = pl.ds(pl.multiple_of(q * LANES, LANES), LANES)
+            total = jnp.sum(sum_wide[span, :], axis=1, keepdims=True)
+            column[pl.ds(q, 1), :] = flat(jnp.broadcast_to(total, (LANES, LANES)))
             return carry
 
         lax.fori_loop(0, col_blocks, across, 0, unroll=2)
@@ -359,76 +390,98 @@
         some = box.at[step, pl.ds(0, count), pl.ds(0, size)]
         pltpu.make_async_copy(some, some, send).wait()
 
-    for step in range(ITERS):
+    def share_rows(step):
+        share(
+            row_box,
+            step,
+            tile,
+            row_box.shape[2] if step == 0 else halves,
+            [(group, lax.rem(tile + r, TILES)) for r in range(1, TILES)],
+            send_sem.at[2 + step],
+            row_sem.at[step],
+        )
+        return row_box[step, :, :halves, :]
+
+    def share_columns(step, own):
+        near_box[step, len(near)] = own
+        share(
+            near_box,
+            step,
+            None,
+            col_blocks,
+            near,
+            send_sem.at[2 + ITERS + step],
+            near_sem.at[step],
+        )
+        return near_box[step]
+
+    with jax.named_scope("row_share"):
+        u = log_cs - merged(share_rows(0))
+    with jax.named_scope("column_pass"):
+        column_lse = first_column_pass(u)
+    told(HOPS)
+    with jax.named_scope("column_share"):
+        lse = merged(share_columns(0, column_lse))
+        v = jnp.where(lse > EMPTY, log_rs - lse, 0.0)
+
+    row_factor = jnp.ones((halves, LANES), jnp.float32)
+    with jax.named_scope("spread"):
+        for q in range(col_blocks):
+            span = pl.ds(q * LANES, LANES)
+            wide = jnp.exp2(top_wide[span, :] + tall(v[q : q + 1, :]))
+            top_wide[span, :] = wide
+            v_wide[span, :] = wide
+    for step in range(1, ITERS):
         last = step + 1 == ITERS
-        if step:
-            with jax.named_scope("row_pass"):
-                row_pass(step)
+        with jax.named_scope("row_pass"):
+            row_box[step, tile, :halves, :] = row_sums()
         with jax.named_scope("row_share"):
-            share(
-                row_box,
-                step,
-                tile,
-                row_box.shape[2] if step == 0 else halves,
-                [(group, lax.rem(tile + r, TILES)) for r in range(1, TILES)],
-                send_sem.at[1 + step],
-                row_sem.at[step],
-            )
-            u = log_cs - merged(row_box[step, :, :halves, :])
+            row_factor = cs_of_row / jnp.sum(share_rows(step), axis=0)
         with jax.named_scope("column_pass"):
-            column_lse = column_pass(u)
+            own = column_sums(row_factor)
         if not last:
-            with jax.named_scope("column_share_near"):
-                near_box[step, len(near)] = column_lse
-                share(
-                    near_box,
-                    step,
-                    None,
-                    col_blocks,
-                    near,
-                    send_sem.at[1 + ITERS + step],
-                    near_sem.at[step],
-                )
-                lse = merged(near_box[step])
-                v = jnp.where(lse > EMPTY, log_rs - lse, 0.0)
-        else:
-            f = (EPS / LOG2E) * u
-            f = f + jnp.concatenate(
-                [row_box[0, t, halves : halves + 2, :] for t in range(TILES)], axis=0
-            ) * (1.0 / depth)
-            size = col_blocks + pair_count
-            y_box[0, y, :col_blocks, :] = column_lse
-            for k in range(pair_count):
-                y_box[0, y, pl.ds(col_blocks + k, 1), :] = jnp.sum(
-                    jnp.where(row_pair == k, f, 0.0), axis=0, keepdims=True
-                )
-            with jax.named_scope("column_share_y"):
-                share(
-                    y_box,
-                    0,
-                    y,
-                    size,
-                    [(in_y(r), tile) for r in range(1, NY)],
-                    send_sem.at[2 * ITERS],
-                    y_sem,
-                )
-                z_box[0, z, :col_blocks, :] = merged(y_box[0, :, :col_blocks, :])
-                z_box[0, z, col_blocks:, :] = jnp.sum(y_box[0, :, col_blocks:, :], axis=0)
-            with jax.named_scope("column_share_z"):
-                share(
-                    z_box,
-                    0,
-                    z,
-                    size,
-                    [(in_z(r), tile) for r in range(1, nz)],
-                    send_sem.at[2 * ITERS + 1],
-                    z_sem,
-                )
-                v = log_rs - merged(z_box[0, :, :col_blocks, :])
-        if not last:
+            with jax.named_scope("column_share"):
+                total = jnp.sum(share_columns(step, own), axis=0)
+                factor = rs_of_col / jnp.maximum(total, 2.0**-60)
             with jax.named_scope("spread"):
                 for q in range(col_blocks):
-                    v_wide[pl.ds(q * LANES, LANES), :] = tall(v[q : q + 1, :])
+                    span = pl.ds(q * LANES, LANES)
+                    v_wide[span, :] = top_wide[span, :] * tall(factor[q : q + 1, :])
+    f = (EPS / LOG2E) * (u + jnp.log2(row_factor))
+    f = f + jnp.concatenate(
+        [row_box[0, t, halves : halves + 2, :] for t in range(TILES)], axis=0
+    ) * (1.0 / depth)
+    size = col_blocks + pair_count
+    y_box[0, y, :col_blocks, :] = jnp.where(
+        own > 0.0, jnp.log2(jnp.maximum(own, TINY)) - v, NEG
+    )
+    for k in range(pair_count):
+        y_box[0, y, pl.ds(col_blocks + k, 1), :] = jnp.sum(
+            jnp.where(row_pair == k, f, 0.0), axis=0, keepdims=True
+        )
+    with jax.named_scope("column_share_y"):
+        share(
+            y_box,
+            0,
+            y,
+            size,
+            [(in_y(r), tile) for r in range(1, NY)],
+            send_sem.at[1 + 2 * ITERS],
+            y_sem,
+        )
+        z_box[0, z, :col_blocks, :] = merged(y_box[0, :, :col_blocks, :])
+        z_box[0, z, col_blocks:, :] = jnp.sum(y_box[0, :, col_blocks:, :], axis=0)
+    with jax.named_scope("column_share_z"):
+        share(
+            z_box,
+            0,
+            z,
+            size,
+            [(in_z(r), tile) for r in range(1, nz)],
+            send_sem.at[2 + 2 * ITERS],
+            z_sem,
+        )
+        v = log_rs - merged(z_box[0, :, :col_blocks, :])
 
     with jax.named_scope("results"):
         g_ref[...] = (EPS / LOG2E) * v + cn[...] * (1.0 / depth)
@@ -445,15 +498,15 @@
         f_ref[...] = value - mean / size_of(own_pair, row_sizes)
 
     with jax.named_scope("sent"):
-        ref = rows.at[pl.ds(0, 7)]
+        ref = rows.at[pl.ds(0, 6)]
         pltpu.make_async_copy(ref, ref, send_sem.at[0]).wait()
         for step in range(ITERS):
             width = row_box.shape[2] if step == 0 else halves
-            sent(row_box, step, TILES - 1, width, send_sem.at[1 + step])
+            sent(row_box, step, TILES - 1, width, send_sem.at[2 + step])
         for step in range(ITERS - 1):
-            sent(near_box, step, len(near), col_blocks, send_sem.at[1 + ITERS + step])
-        sent(y_box, 0, NY - 1, size, send_sem.at[2 * ITERS])
-        sent(z_box, 0, nz - 1, size, send_sem.at[2 * ITERS + 1])
+            sent(near_box, step, len(near), col_blocks, send_sem.at[2 + ITERS + step])
+        sent(y_box, 0, NY - 1, size, send_sem.at[1 + 2 * ITERS])
+        sent(z_box, 0, nz - 1, size, send_sem.at[2 + 2 * ITERS])
 
 
 def local(candidates, validation, row_sizes, col_sizes):
@@ -492,8 +545,9 @@
             pltpu.VMEM((1, NY, col_blocks + pairs, LANES), jnp.float32),
             pltpu.VMEM((1, groups // NY, col_blocks + pairs, LANES), jnp.float32),
             pltpu.SemaphoreType.DMA((4,)),
-            pltpu.SemaphoreType.DMA((2 * ITERS + 2,)),
+            pltpu.SemaphoreType.DMA((2 * ITERS + 3,)),
             pltpu.SemaphoreType.DMA((7, 2)),
+            pltpu.SemaphoreType.REGULAR((HOPS,)),
             pltpu.SemaphoreType.DMA((ITERS,)),
             pltpu.SemaphoreType.DMA((ITERS - 1,)),
             pltpu.SemaphoreType.DMA,

time: 91.4 us -> 83.8 us (0.917)
  Pallas kernels: 88.1 us -> 80.5 us
    pallas_call x1, Pallas kernels: 88.1 us -> 80.5 us  [local(): pl.pallas_call(functools.partial(kernel, pairs, groups), out_shape=(jax.S...]
where the time goes in v3:
time: 83.8 us; the launch traced here: 83.6 us
  Pallas kernels  80.5 us (96%)
  local copies, waits for them, and re-layouts  2.48 us (3%)
    pallas_call x1, Pallas kernels, local(): pl.pallas_call(functools.partial(kernel, pairs, groups), out_shape=(jax.S...  80.5 us
    unnamed x2, local copies, waits for them, and re-layouts  2.48 us

profile of v3, /device:TPU:1, one launch (start us, length us, event | category | flops | bytes accessed | tf_op | source)
XLA Modules:
  0.0 83.6 jit_solution(613222880652088548)
XLA Ops:
  0.6 80.5 %shard_map.59 = (f32[2,128]{1,0:T(2,128)}, f32[8,128]{1,0:T(8,128)}) custom-call(s32[16]{0:T(128)} %rs_hbm.1, s32[16]{0:T(128)} %cs_hbm.1, bf16[256,768]{1,0:T(8,128)(2,1)} %x_ref.1, bf16[1024,768]{1,0:T(8,128)(2,1)} %y_hbm.1), custom_call_target="tpu_custom_call" | custom-call | tf_op jit(solution)/shard_map/pallas_call | solution.py:523
  81.1 1.2 %copy.8 = f32[256]{0:T(256)} copy(f32[256]{0:T(256)} %bitcast.3) | data formatting | bytes 2048
  82.3 1.3 %copy.9 = f32[1024]{0:T(1024)} copy(f32[1024]{0:T(1024)} %bitcast.2) | data formatting | bytes 8192

commit v4 on v3

--- a/solution.py
+++ b/solution.py
@@ -18,6 +18,7 @@
 TILES = 2 * NX
 ROW_MOST = 24576
 HOPS = 4
+TILE_ORDER = ((2, 0), (2, 1), (1, 1), (3, 1), (1, 0), (3, 0), (0, 1))
 LANES = 128
 MESH = pl.DeviceIdType.MESH
 
@@ -100,7 +101,8 @@
         return lax.rem(z + r, nz) * NY + y
 
     with jax.named_scope("greet"):
-        near = [(lax.rem(group + r + group_count, group_count), tile) for r in range(-reach, reach + 1) if r]
+        offsets = sorted((r for r in range(-reach, reach + 1) if r), key=lambda r: -abs(r))
+        near = [(lax.rem(group + r + group_count, group_count), tile) for r in offsets]
         neighbours = [(in_y(1), tile), (in_y(NY - 1), tile), (in_z(1), tile), (in_z(nz - 1), tile)]
         copies = [
             pltpu.make_async_copy(a, b, local_sem.at[i])
@@ -123,12 +125,12 @@
     def told(r):
         pl.semaphore_wait(hop_sem.at[r - 1], len(neighbours))
 
-    def send_block(block, part, to, sem, sent=0):
+    def send_block(block, part, to, sem):
         ref = rows.at[block, pl.ds(part * half, half)]
         copy = pltpu.make_async_remote_copy(
             src_ref=ref,
             dst_ref=ref,
-            send_sem=send_sem.at[sent],
+            send_sem=send_sem.at[0],
             recv_sem=block_sem.at[sem, part],
             device_id=(group, to),
             device_id_type=MESH,
@@ -143,8 +145,8 @@
     right, left, sib = at(1, False), at(NX - 1, False), at(0, True)
 
     with jax.named_scope("send_own"):
-        send_block(tile, 0, right, LEFT, 1)
-        send_block(tile, 1, left, RIGHT, 1)
+        send_block(tile, 0, right, LEFT)
+        send_block(tile, 1, left, RIGHT)
         send_block(tile, 0, sib, SIB)
         send_block(tile, 1, sib, SIB)
         tell(1)
@@ -211,17 +213,16 @@
                 (((1,), (1,)), ((), ())),
                 preferred_element_type=jnp.float32,
             )
-            v = v_wide[span, :]
+            v = v_wide[span, :].reshape(chunk // 8, 8, LANES)
             col_pair = pair_wide[span, :]
             new = []
             for h in range(2):
                 k = jnp.where(
                     col_pair == block_pair[h], cross[:, h * half : (h + 1) * half] * scale, NEG
                 )
-                scores[2 * block + h, span, :] = k
-                new.append(
-                    jnp.maximum(top[h], jnp.max((k + v).reshape(chunk // 8, 8, LANES), axis=0))
-                )
+                k = k.reshape(chunk // 8, 8, LANES)
+                scores[pl.ds(i * (chunk // 8), chunk // 8), 2 * block + h] = k
+                new.append(jnp.maximum(top[h], jnp.max(k + v, axis=0)))
             return tuple(new)
 
         start = jnp.full((8, LANES), 4 * NEG, jnp.float32)
@@ -230,11 +231,11 @@
 
         def total(i, so_far):
             span = pl.ds(pl.multiple_of(i * LANES, LANES), LANES)
-            v = v_wide[span, :]
+            v = v_wide[span, :].reshape(LANES // 8, 8, LANES)
             new = []
             for h in range(2):
-                e = jnp.exp2(scores[2 * block + h, span, :] + v - top[h])
-                new.append(so_far[h] + jnp.sum(e.reshape(LANES // 8, 8, LANES), axis=0))
+                k = scores[pl.ds(i * (LANES // 8), LANES // 8), 2 * block + h]
+                new.append(so_far[h] + jnp.sum(jnp.exp2(k + v - top[h][None]), axis=0))
             return tuple(new)
 
         start = jnp.zeros((8, LANES), jnp.float32)
@@ -249,14 +250,11 @@
 
     with jax.named_scope("scores_near"):
         score_blocks(0, False)
+        send_block(tile, 1, right, LEFT)
+        send_block(tile, 0, left, RIGHT)
         wait_half(SIB, 0)
         wait_half(SIB, 1)
         score_blocks(0, True)
-
-    with jax.named_scope("send_own_rest"):
-        pltpu.make_async_copy(rows.at[0], rows.at[0], send_sem.at[1]).wait()
-        send_block(tile, 1, right, LEFT)
-        send_block(tile, 0, left, RIGHT)
         told(1)
         tell(2)
 
@@ -319,7 +317,7 @@
     def row_sums():
         def add(i, so_far):
             span = pl.ds(pl.multiple_of(i * 8, 8), 8)
-            return so_far + scores[:, span, :] * v_wide[span, :][None]
+            return so_far + scores[i] * v_wide[span, :][None]
 
         start = jnp.zeros((halves, 8, LANES), jnp.float32)
         return jnp.sum(lax.fori_loop(0, n_col // 8, add, start, unroll=4), axis=1)
@@ -329,10 +327,10 @@
 
         def lanes(i, carry):
             span = pl.ds(pl.multiple_of(i * 8, 8), 8)
-            t = scores[:, span, :] + u_wide
+            t = scores[i] + u_wide
             top = jnp.max(t, axis=0)
             e = jnp.exp2(t - top[None])
-            scores[:, span, :] = e
+            scores[i] = e
             top_wide[span, :] = top
             sum_wide[span, :] = jnp.sum(e, axis=0)
             return carry
@@ -355,21 +353,20 @@
 
     def column_sums(b):
         b_wide = jnp.broadcast_to(b[:, None, :], (halves, 8, LANES))
-
-        def lanes(i, carry):
-            span = pl.ds(pl.multiple_of(i * 8, 8), 8)
-            sum_wide[span, :] = jnp.sum(scores[:, span, :] * b_wide, axis=0) * top_wide[span, :]
+        groups = LANES // 8
+
+        def some(q, carry):
+            flat_sum = jnp.zeros((8, LANES), jnp.float32)
+            for j in range(groups):
+                i = q * groups + j
+                span = pl.ds(pl.multiple_of(i * 8, 8), 8)
+                lanes = jnp.sum(scores[i] * b_wide, axis=0) * top_wide[span, :]
+                total = jnp.broadcast_to(jnp.sum(lanes, axis=1, keepdims=True), (8, LANES))
+                flat_sum = jnp.where(eye[8 * j : 8 * j + 8], total, flat_sum)
+            column[pl.ds(q, 1), :] = jnp.sum(flat_sum, axis=0, keepdims=True)
             return carry
 
-        lax.fori_loop(0, n_col // 8, lanes, 0, unroll=4)
-
-        def across(q, carry):
-            span = pl.ds(pl.multiple_of(q * LANES, LANES), LANES)
-            total = jnp.sum(sum_wide[span, :], axis=1, keepdims=True)
-            column[pl.ds(q, 1), :] = flat(jnp.broadcast_to(total, (LANES, LANES)))
-            return carry
-
-        lax.fori_loop(0, col_blocks, across, 0, unroll=2)
+        lax.fori_loop(0, col_blocks, some, 0)
         return column[...]
 
     def share(box, step, me, size, targets, send, recv):
@@ -396,7 +393,7 @@
             step,
             tile,
             row_box.shape[2] if step == 0 else halves,
-            [(group, lax.rem(tile + r, TILES)) for r in range(1, TILES)],
+            [(group, at(dx, flip)) for dx, flip in TILE_ORDER],
             send_sem.at[2 + step],
             row_sem.at[step],
         )
@@ -451,33 +448,37 @@
     f = f + jnp.concatenate(
         [row_box[0, t, halves : halves + 2, :] for t in range(TILES)], axis=0
     ) * (1.0 / depth)
-    size = col_blocks + pair_count
+    size = col_blocks + 1
     y_box[0, y, :col_blocks, :] = jnp.where(
         own > 0.0, jnp.log2(jnp.maximum(own, TINY)) - v, NEG
     )
-    for k in range(pair_count):
-        y_box[0, y, pl.ds(col_blocks + k, 1), :] = jnp.sum(
-            jnp.where(row_pair == k, f, 0.0), axis=0, keepdims=True
-        )
+    sums = jnp.concatenate(
+        [jnp.sum(jnp.where(row_pair == k, f, 0.0), axis=0, keepdims=True) for k in range(pair_count)],
+        axis=0,
+    )
+    sums = jnp.broadcast_to(jnp.sum(sums, axis=1, keepdims=True), (pair_count, LANES))
+    y_box[0, y, pl.ds(col_blocks, 1), :] = jnp.sum(
+        jnp.where(eye[:pair_count], sums, 0.0), axis=0, keepdims=True
+    )
     with jax.named_scope("column_share_y"):
         share(
             y_box,
             0,
             y,
             size,
-            [(in_y(r), tile) for r in range(1, NY)],
+            [(in_y(r), tile) for r in sorted(range(1, NY), key=lambda r: -min(r, NY - r))],
             send_sem.at[1 + 2 * ITERS],
             y_sem,
         )
         z_box[0, z, :col_blocks, :] = merged(y_box[0, :, :col_blocks, :])
-        z_box[0, z, col_blocks:, :] = jnp.sum(y_box[0, :, col_blocks:, :], axis=0)
+        z_box[0, z, pl.ds(col_blocks, 1), :] = jnp.sum(y_box[0, :, col_blocks:size, :], axis=0)
     with jax.named_scope("column_share_z"):
         share(
             z_box,
             0,
             z,
             size,
-            [(in_z(r), tile) for r in range(1, nz)],
+            [(in_z(r), tile) for r in sorted(range(1, nz), key=lambda r: -min(r, nz - r))],
             send_sem.at[2 + 2 * ITERS],
             z_sem,
         )
@@ -485,8 +486,7 @@
 
     with jax.named_scope("results"):
         g_ref[...] = (EPS / LOG2E) * v + cn[...] * (1.0 / depth)
-        sums = jnp.sum(z_box[0, :, col_blocks:, :], axis=0)
-        sums = jnp.broadcast_to(jnp.sum(sums, axis=1, keepdims=True), (pair_count, LANES))
+        sums = tall(jnp.sum(z_box[0, :, col_blocks:size, :], axis=0))
         value = jnp.zeros((2, LANES), jnp.float32)
         own_pair = jnp.zeros((2, LANES), jnp.int32)
         for t in range(TILES):
@@ -498,7 +498,7 @@
         f_ref[...] = value - mean / size_of(own_pair, row_sizes)
 
     with jax.named_scope("sent"):
-        ref = rows.at[pl.ds(0, 6)]
+        ref = rows.at[pl.ds(0, 7)]
         pltpu.make_async_copy(ref, ref, send_sem.at[0]).wait()
         for step in range(ITERS):
             width = row_box.shape[2] if step == 0 else halves
@@ -533,7 +533,7 @@
             pltpu.SMEM((pairs,), jnp.int32),
             pltpu.VMEM((n_col, depth), jnp.bfloat16),
             pltpu.VMEM((TILES, n_row, depth), jnp.bfloat16),
-            pltpu.VMEM((halves, n_col, half), jnp.float32),
+            pltpu.VMEM((n_col // 8, halves, 8, half), jnp.float32),
             pltpu.VMEM((n_col, LANES), jnp.float32),
             pltpu.VMEM((n_col, LANES), jnp.int32),
             pltpu.VMEM((n_col, LANES), jnp.float32),
@@ -542,8 +542,8 @@
             pltpu.VMEM((col_blocks, LANES), jnp.float32),
             pltpu.VMEM((ITERS, TILES, halves + 8, half), jnp.float32),
             pltpu.VMEM((ITERS - 1, near + 1, col_blocks, LANES), jnp.float32),
-            pltpu.VMEM((1, NY, col_blocks + pairs, LANES), jnp.float32),
-            pltpu.VMEM((1, groups // NY, col_blocks + pairs, LANES), jnp.float32),
+            pltpu.VMEM((1, NY, col_blocks + 8, LANES), jnp.float32),
+            pltpu.VMEM((1, groups // NY, col_blocks + 8, LANES), jnp.float32),
             pltpu.SemaphoreType.DMA((4,)),
             pltpu.SemaphoreType.DMA((2 * ITERS + 3,)),
             pltpu.SemaphoreType.DMA((7, 2)),

time: 83.8 us -> 75.6 us (0.902)
  Pallas kernels: 80.5 us -> 71.9 us
    pallas_call x1, Pallas kernels: 80.5 us -> 71.9 us  [local(): pl.pallas_call(functools.partial(kernel, pairs, groups), out_shape=(jax.S...]
where the time goes in v4:
time: 75.6 us; the launch traced here: 75 us
  Pallas kernels  71.9 us (95%)
  local copies, waits for them, and re-layouts  2.48 us (3%)
    pallas_call x1, Pallas kernels, local(): pl.pallas_call(functools.partial(kernel, pairs, groups), out_shape=(jax.S...  71.9 us
    unnamed x2, local copies, waits for them, and re-layouts  2.48 us

profile of v4, /device:TPU:1, one launch (start us, length us, event | category | flops | bytes accessed | tf_op | source)
XLA Modules:
  0.0 75.0 jit_solution(2739125146733449935)
XLA Ops:
  0.6 71.9 %shard_map.59 = (f32[2,128]{1,0:T(2,128)}, f32[8,128]{1,0:T(8,128)}) custom-call(s32[16]{0:T(128)} %rs_hbm.1, s32[16]{0:T(128)} %cs_hbm.1, bf16[256,768]{1,0:T(8,128)(2,1)} %x_ref.1, bf16[1024,768]{1,0:T(8,128)(2,1)} %y_hbm.1), custom_call_target="tpu_custom_call" | custom-call | tf_op jit(solution)/shard_map/pallas_call | solution.py:523
  72.5 1.2 %copy.8 = f32[256]{0:T(256)} copy(f32[256]{0:T(256)} %bitcast.3) | data formatting | bytes 2048
  73.7 1.3 %copy.9 = f32[1024]{0:T(1024)} copy(f32[1024]{0:T(1024)} %bitcast.2) | data formatting | bytes 8192

commit v5 on v4

--- a/solution.py
+++ b/solution.py
@@ -78,6 +78,7 @@
     n_row, depth = x_ref.shape
     n_col = y_ref.shape[0]
     half = n_row // 2
+    quarter = n_row // 4
     halves = 2 * TILES
     col_blocks = n_col // LANES
     nz = group_count // NY
@@ -125,30 +126,29 @@
     def told(r):
         pl.semaphore_wait(hop_sem.at[r - 1], len(neighbours))
 
-    def send_block(block, part, to, sem):
-        ref = rows.at[block, pl.ds(part * half, half)]
-        copy = pltpu.make_async_remote_copy(
+    def send(block, part, count, to, sem):
+        ref = rows.at[block, pl.ds(part * quarter, count * quarter)]
+        pltpu.make_async_remote_copy(
             src_ref=ref,
             dst_ref=ref,
             send_sem=send_sem.at[0],
             recv_sem=block_sem.at[sem, part],
             device_id=(group, to),
             device_id_type=MESH,
-        )
-        copy.start()
-
-    def wait_half(sem, part):
-        ref = rows.at[0, pl.ds(0, half)]
+        ).start()
+
+    def arrived(sem, part, count):
+        ref = rows.at[0, pl.ds(0, count * quarter)]
         pltpu.make_async_copy(ref, ref, block_sem.at[sem, part]).wait()
 
     SIB, LEFT, RIGHT, LEFT_SIB, RIGHT_SIB, OPP, OPP_SIB = range(7)
     right, left, sib = at(1, False), at(NX - 1, False), at(0, True)
 
     with jax.named_scope("send_own"):
-        send_block(tile, 0, right, LEFT)
-        send_block(tile, 1, left, RIGHT)
-        send_block(tile, 0, sib, SIB)
-        send_block(tile, 1, sib, SIB)
+        for i in range(2):
+            send(tile, i, 1, right, LEFT)
+            send(tile, 3 - i, 1, left, RIGHT)
+        send(tile, 0, 4, sib, SIB)
         tell(1)
 
     with jax.named_scope("inputs"):
@@ -197,7 +197,7 @@
             squares(rows[tile, pl.ds(h * half, half), :])
         )
 
-    chunk = min(512, n_col)
+    chunk = min(1024, n_col)
 
     def score_block(block):
         first = group * (n_row * TILES) + block * n_row
@@ -239,7 +239,7 @@
             return tuple(new)
 
         start = jnp.zeros((8, LANES), jnp.float32)
-        sums = lax.fori_loop(0, n_col // LANES, total, (start, start))
+        sums = lax.fori_loop(0, n_col // LANES, total, (start, start), unroll=4)
         for h in range(2):
             row_box[0, tile, pl.ds(2 * block + h, 1), :] = top[h] + jnp.log2(
                 jnp.sum(sums[h], axis=0, keepdims=True)
@@ -250,10 +250,9 @@
 
     with jax.named_scope("scores_near"):
         score_blocks(0, False)
-        send_block(tile, 1, right, LEFT)
-        send_block(tile, 0, left, RIGHT)
-        wait_half(SIB, 0)
-        wait_half(SIB, 1)
+        send(tile, 2, 2, right, LEFT)
+        send(tile, 0, 2, left, RIGHT)
+        arrived(SIB, 0, 4)
         score_blocks(0, True)
         told(1)
         tell(2)
@@ -261,16 +260,17 @@
     left_block, right_block = at(NX - 1, False), at(1, False)
     opposite = at(2, False)
     with jax.named_scope("forward"):
-        wait_half(LEFT, 0)
-        send_block(left_block, 0, right, OPP)
-        send_block(left_block, 0, sib, LEFT_SIB)
-        wait_half(RIGHT, 1)
-        send_block(right_block, 1, left, OPP)
-        send_block(right_block, 1, sib, RIGHT_SIB)
-        wait_half(LEFT, 1)
-        send_block(left_block, 1, sib, LEFT_SIB)
-        wait_half(RIGHT, 0)
-        send_block(right_block, 0, sib, RIGHT_SIB)
+        for i in range(2):
+            arrived(LEFT, i, 1)
+            send(left_block, i, 1, right, OPP)
+            arrived(RIGHT, 3 - i, 1)
+            send(right_block, 3 - i, 1, left, OPP)
+        send(left_block, 0, 2, sib, LEFT_SIB)
+        send(right_block, 2, 2, sib, RIGHT_SIB)
+        arrived(LEFT, 2, 2)
+        send(left_block, 2, 2, sib, LEFT_SIB)
+        arrived(RIGHT, 0, 2)
+        send(right_block, 0, 2, sib, RIGHT_SIB)
         told(2)
         tell(3)
 
@@ -281,9 +281,9 @@
             return carry
 
         lax.fori_loop(0, 2, side, 0)
-        for part in range(2):
-            wait_half(LEFT_SIB, part)
-            wait_half(RIGHT_SIB, part)
+        for part in (0, 2):
+            arrived(LEFT_SIB, part, 2)
+            arrived(RIGHT_SIB, part, 2)
 
         def other_side(s, carry):
             score_block(2 * lax.rem(x + 1 + 2 * s, NX) + 1 - core)
@@ -294,13 +294,13 @@
         tell(4)
 
     with jax.named_scope("wait_opposite"):
-        for part in range(2):
-            wait_half(OPP, part)
-            send_block(opposite, part, sib, OPP_SIB)
+        for part in (0, 3, 1, 2):
+            arrived(OPP, part, 1)
+            send(opposite, part, 1, sib, OPP_SIB)
     with jax.named_scope("scores_opposite"):
         score_blocks(2, False)
-        for part in range(2):
-            wait_half(OPP_SIB, part)
+        for part in (0, 3, 1, 2):
+            arrived(OPP_SIB, part, 1)
         score_blocks(2, True)
 
     row_line = lax.broadcasted_iota(jnp.int32, (halves, LANES), 0)
@@ -348,25 +348,26 @@
             )
             return carry
 
-        lax.fori_loop(0, col_blocks, across, 0, unroll=2)
+        lax.fori_loop(0, col_blocks, across, 0, unroll=True)
         return column[...]
 
     def column_sums(b):
         b_wide = jnp.broadcast_to(b[:, None, :], (halves, 8, LANES))
-        groups = LANES // 8
-
-        def some(q, carry):
-            flat_sum = jnp.zeros((8, LANES), jnp.float32)
-            for j in range(groups):
-                i = q * groups + j
-                span = pl.ds(pl.multiple_of(i * 8, 8), 8)
-                lanes = jnp.sum(scores[i] * b_wide, axis=0) * top_wide[span, :]
-                total = jnp.broadcast_to(jnp.sum(lanes, axis=1, keepdims=True), (8, LANES))
-                flat_sum = jnp.where(eye[8 * j : 8 * j + 8], total, flat_sum)
-            column[pl.ds(q, 1), :] = jnp.sum(flat_sum, axis=0, keepdims=True)
-            return carry
-
-        lax.fori_loop(0, col_blocks, some, 0)
+
+        def lanes(i, carry):
+            span = pl.ds(pl.multiple_of(i * 8, 8), 8)
+            sum_wide[span, :] = jnp.sum(scores[i] * b_wide, axis=0) * top_wide[span, :]
+            return carry
+
+        lax.fori_loop(0, n_col // 8, lanes, 0, unroll=4)
+
+        def across(q, carry):
+            span = pl.ds(pl.multiple_of(q * LANES, LANES), LANES)
+            total = jnp.sum(sum_wide[span, :], axis=1, keepdims=True)
+            column[pl.ds(q, 1), :] = flat(jnp.broadcast_to(total, (LANES, LANES)))
+            return carry
+
+        lax.fori_loop(0, col_blocks, across, 0, unroll=True)
         return column[...]
 
     def share(box, step, me, size, targets, send, recv):
@@ -546,7 +547,7 @@
             pltpu.VMEM((1, groups // NY, col_blocks + 8, LANES), jnp.float32),
             pltpu.SemaphoreType.DMA((4,)),
             pltpu.SemaphoreType.DMA((2 * ITERS + 3,)),
-            pltpu.SemaphoreType.DMA((7, 2)),
+            pltpu.SemaphoreType.DMA((7, 4)),
             pltpu.SemaphoreType.REGULAR((HOPS,)),
             pltpu.SemaphoreType.DMA((ITERS,)),
             pltpu.SemaphoreType.DMA((ITERS - 1,)),

time: 75.6 us -> 73.5 us (0.972)
  Pallas kernels: 71.9 us -> 69.8 us
    pallas_call x1, Pallas kernels: 71.9 us -> 69.8 us  [local(): pl.pallas_call(functools.partial(kernel, pairs, groups), out_shape=(jax.S...]
where the time goes in v5:
time: 73.5 us; the launch traced here: 73 us
  Pallas kernels  69.8 us (95%)
  local copies, waits for them, and re-layouts  2.48 us (3%)
    pallas_call x1, Pallas kernels, local(): pl.pallas_call(functools.partial(kernel, pairs, groups), out_shape=(jax.S...  69.8 us
    unnamed x2, local copies, waits for them, and re-layouts  2.48 us

profile of v5, /device:TPU:1, one launch (start us, length us, event | category | flops | bytes accessed | tf_op | source)
XLA Modules:
  0.0 73.0 jit_solution(15668893670517984222)
XLA Ops:
  0.6 69.8 %shard_map.59 = (f32[2,128]{1,0:T(2,128)}, f32[8,128]{1,0:T(8,128)}) custom-call(s32[16]{0:T(128)} %rs_hbm.1, s32[16]{0:T(128)} %cs_hbm.1, bf16[256,768]{1,0:T(8,128)(2,1)} %x_ref.1, bf16[1024,768]{1,0:T(8,128)(2,1)} %y_hbm.1), custom_call_target="tpu_custom_call" | custom-call | tf_op jit(solution)/shard_map/pallas_call | solution.py:524
  70.5 1.2 %copy.8 = f32[256]{0:T(256)} copy(f32[256]{0:T(256)} %bitcast.3) | data formatting | bytes 2048
  71.7 1.3 %copy.9 = f32[1024]{0:T(1024)} copy(f32[1024]{0:T(1024)} %bitcast.2) | data formatting | bytes 8192

commit v6 on v5

--- a/solution.py
+++ b/solution.py
@@ -263,10 +263,10 @@
         for i in range(2):
             arrived(LEFT, i, 1)
             send(left_block, i, 1, right, OPP)
+            send(left_block, i, 1, sib, LEFT_SIB)
             arrived(RIGHT, 3 - i, 1)
             send(right_block, 3 - i, 1, left, OPP)
-        send(left_block, 0, 2, sib, LEFT_SIB)
-        send(right_block, 2, 2, sib, RIGHT_SIB)
+            send(right_block, 3 - i, 1, sib, RIGHT_SIB)
         arrived(LEFT, 2, 2)
         send(left_block, 2, 2, sib, LEFT_SIB)
         arrived(RIGHT, 0, 2)
@@ -281,9 +281,11 @@
             return carry
 
         lax.fori_loop(0, 2, side, 0)
-        for part in (0, 2):
-            arrived(LEFT_SIB, part, 2)
-            arrived(RIGHT_SIB, part, 2)
+        for i in range(2):
+            arrived(LEFT_SIB, i, 1)
+            arrived(RIGHT_SIB, 3 - i, 1)
+        arrived(LEFT_SIB, 2, 2)
+        arrived(RIGHT_SIB, 0, 2)
 
         def other_side(s, carry):
             score_block(2 * lax.rem(x + 1 + 2 * s, NX) + 1 - core)
@@ -320,7 +322,7 @@
             return so_far + scores[i] * v_wide[span, :][None]
 
         start = jnp.zeros((halves, 8, LANES), jnp.float32)
-        return jnp.sum(lax.fori_loop(0, n_col // 8, add, start, unroll=4), axis=1)
+        return jnp.sum(lax.fori_loop(0, n_col // 8, add, start, unroll=16), axis=1)
 
     def first_column_pass(u):
         u_wide = jnp.broadcast_to(u[:, None, :], (halves, 8, LANES))
@@ -359,7 +361,7 @@
             sum_wide[span, :] = jnp.sum(scores[i] * b_wide, axis=0) * top_wide[span, :]
             return carry
 
-        lax.fori_loop(0, n_col // 8, lanes, 0, unroll=4)
+        lax.fori_loop(0, n_col // 8, lanes, 0, unroll=16)
 
         def across(q, carry):
             span = pl.ds(pl.multiple_of(q * LANES, LANES), LANES)
@@ -393,7 +395,7 @@
             row_box,
             step,
             tile,
-            row_box.shape[2] if step == 0 else halves,
+            halves + 2 if step == 0 else halves,
             [(group, at(dx, flip)) for dx, flip in TILE_ORDER],
             send_sem.at[2 + step],
             row_sem.at[step],
@@ -502,7 +504,7 @@
         ref = rows.at[pl.ds(0, 7)]
         pltpu.make_async_copy(ref, ref, send_sem.at[0]).wait()
         for step in range(ITERS):
-            width = row_box.shape[2] if step == 0 else halves
+            width = halves + 2 if step == 0 else halves
             sent(row_box, step, TILES - 1, width, send_sem.at[2 + step])
         for step in range(ITERS - 1):
             sent(near_box, step, len(near), col_blocks, send_sem.at[2 + ITERS + step])

time: 73.5 us -> 72.7 us (0.989)
  Pallas kernels: 69.8 us -> 68.9 us
    pallas_call x1, Pallas kernels: 69.8 us -> 68.9 us  [local(): pl.pallas_call(functools.partial(kernel, pairs, groups), out_shape=(jax.S...]
where the time goes in v6:
time: 72.7 us; the launch traced here: 72 us
  Pallas kernels  68.9 us (95%)
  local copies, waits for them, and re-layouts  2.48 us (3%)
    pallas_call x1, Pallas kernels, local(): pl.pallas_call(functools.partial(kernel, pairs, groups), out_shape=(jax.S...  68.9 us
    unnamed x2, local copies, waits for them, and re-layouts  2.48 us

profile of v6, /device:TPU:1, one launch (start us, length us, event | category | flops | bytes accessed | tf_op | source)
XLA Modules:
  0.0 72.0 jit_solution(987689707858758590)
XLA Ops:
  0.6 68.9 %shard_map.59 = (f32[2,128]{1,0:T(2,128)}, f32[8,128]{1,0:T(8,128)}) custom-call(s32[16]{0:T(128)} %rs_hbm.1, s32[16]{0:T(128)} %cs_hbm.1, bf16[256,768]{1,0:T(8,128)(2,1)} %x_ref.1, bf16[1024,768]{1,0:T(8,128)(2,1)} %y_hbm.1), custom_call_target="tpu_custom_call" | custom-call | tf_op jit(solution)/shard_map/pallas_call | solution.py:526
  69.5 1.2 %copy.8 = f32[256]{0:T(256)} copy(f32[256]{0:T(256)} %bitcast.3) | data formatting | bytes 2048
  70.8 1.3 %copy.9 = f32[1024]{0:T(1024)} copy(f32[1024]{0:T(1024)} %bitcast.2) | data formatting | bytes 8192

commit v7 on v6

--- a/solution.py
+++ b/solution.py
@@ -73,6 +73,7 @@
     row_sem,
     near_sem,
     y_sem,
+    sum_sem,
     z_sem,
 ):
     n_row, depth = x_ref.shape
@@ -372,7 +373,7 @@
         lax.fori_loop(0, col_blocks, across, 0, unroll=True)
         return column[...]
 
-    def share(box, step, me, size, targets, send, recv):
+    def share(box, step, me, size, targets, send, recv, meanwhile=lambda: None):
         own = box.at[step, len(targets) if me is None else me, pl.ds(0, size)]
         for i, to in enumerate(targets):
             pltpu.make_async_remote_copy(
@@ -383,8 +384,10 @@
                 device_id=to,
                 device_id_type=MESH,
             ).start()
+        made = meanwhile()
         some = box.at[step, pl.ds(0, len(targets)), pl.ds(0, size)]
         pltpu.make_async_copy(some, some, recv).wait()
+        return made
 
     def sent(box, step, count, size, send):
         some = box.at[step, pl.ds(0, count), pl.ds(0, size)]
@@ -447,32 +450,50 @@
                 for q in range(col_blocks):
                     span = pl.ds(q * LANES, LANES)
                     v_wide[span, :] = top_wide[span, :] * tall(factor[q : q + 1, :])
-    f = (EPS / LOG2E) * (u + jnp.log2(row_factor))
-    f = f + jnp.concatenate(
-        [row_box[0, t, halves : halves + 2, :] for t in range(TILES)], axis=0
-    ) * (1.0 / depth)
     size = col_blocks + 1
     y_box[0, y, :col_blocks, :] = jnp.where(
         own > 0.0, jnp.log2(jnp.maximum(own, TINY)) - v, NEG
     )
-    sums = jnp.concatenate(
-        [jnp.sum(jnp.where(row_pair == k, f, 0.0), axis=0, keepdims=True) for k in range(pair_count)],
-        axis=0,
-    )
-    sums = jnp.broadcast_to(jnp.sum(sums, axis=1, keepdims=True), (pair_count, LANES))
-    y_box[0, y, pl.ds(col_blocks, 1), :] = jnp.sum(
-        jnp.where(eye[:pair_count], sums, 0.0), axis=0, keepdims=True
-    )
+    y_targets = [(in_y(r), tile) for r in sorted(range(1, NY), key=lambda r: -min(r, NY - r))]
+
+    def pair_sums():
+        f = (EPS / LOG2E) * (u + jnp.log2(row_factor))
+        f = f + jnp.concatenate(
+            [row_box[0, t, halves : halves + 2, :] for t in range(TILES)], axis=0
+        ) * (1.0 / depth)
+        sums = jnp.concatenate(
+            [jnp.sum(jnp.where(row_pair == k, f, 0.0), axis=0, keepdims=True) for k in range(pair_count)],
+            axis=0,
+        )
+        sums = jnp.broadcast_to(jnp.sum(sums, axis=1, keepdims=True), (pair_count, LANES))
+        y_box[0, y, pl.ds(col_blocks, 1), :] = jnp.sum(
+            jnp.where(eye[:pair_count], sums, 0.0), axis=0, keepdims=True
+        )
+        mine = y_box.at[0, y, pl.ds(col_blocks, 1)]
+        for to in y_targets:
+            pltpu.make_async_remote_copy(
+                src_ref=mine,
+                dst_ref=mine,
+                send_sem=send_sem.at[1],
+                recv_sem=sum_sem,
+                device_id=to,
+                device_id_type=MESH,
+            ).start()
+        return f
+
     with jax.named_scope("column_share_y"):
-        share(
+        f = share(
             y_box,
             0,
             y,
-            size,
-            [(in_y(r), tile) for r in sorted(range(1, NY), key=lambda r: -min(r, NY - r))],
+            col_blocks,
+            y_targets,
             send_sem.at[1 + 2 * ITERS],
             y_sem,
-        )
+            pair_sums,
+        )
+        some = y_box.at[0, pl.ds(0, NY - 1), pl.ds(col_blocks, 1)]
+        pltpu.make_async_copy(some, some, sum_sem).wait()
         z_box[0, z, :col_blocks, :] = merged(y_box[0, :, :col_blocks, :])
         z_box[0, z, pl.ds(col_blocks, 1), :] = jnp.sum(y_box[0, :, col_blocks:size, :], axis=0)
     with jax.named_scope("column_share_z"):
@@ -508,7 +529,8 @@
             sent(row_box, step, TILES - 1, width, send_sem.at[2 + step])
         for step in range(ITERS - 1):
             sent(near_box, step, len(near), col_blocks, send_sem.at[2 + ITERS + step])
-        sent(y_box, 0, NY - 1, size, send_sem.at[1 + 2 * ITERS])
+        sent(y_box, 0, NY - 1, col_blocks, send_sem.at[1 + 2 * ITERS])
+        pltpu.make_async_copy(some, some, send_sem.at[1]).wait()
         sent(z_box, 0, nz - 1, size, send_sem.at[2 + 2 * ITERS])
 
 
@@ -555,6 +577,7 @@
             pltpu.SemaphoreType.DMA((ITERS - 1,)),
             pltpu.SemaphoreType.DMA,
             pltpu.SemaphoreType.DMA,
+            pltpu.SemaphoreType.DMA,
         ],
         compiler_params=pltpu.CompilerParams(
             collective_id=0, has_side_effects=True, vmem_limit_bytes=56 * 2**20

time: 72.7 us -> 72.8 us (level)
  no operation moved by 1% of the time
where the time goes in v7:
time: 72.8 us; the launch traced here: 72.2 us
  Pallas kernels  69 us (95%)
  local copies, waits for them, and re-layouts  2.48 us (3%)
    pallas_call x1, Pallas kernels, local(): pl.pallas_call(functools.partial(kernel, pairs, groups), out_shape=(jax.S...  69 us
    unnamed x2, local copies, waits for them, and re-layouts  2.48 us

profile of v7, /device:TPU:1, one launch (start us, length us, event | category | flops | bytes accessed | tf_op | source)
XLA Modules:
  0.0 72.2 jit_solution(13750320987340148949)
XLA Ops:
  0.6 69.0 %shard_map.59 = (f32[2,128]{1,0:T(2,128)}, f32[8,128]{1,0:T(8,128)}) custom-call(s32[16]{0:T(128)} %rs_hbm.1, s32[16]{0:T(128)} %cs_hbm.1, bf16[256,768]{1,0:T(8,128)(2,1)} %x_ref.1, bf16[1024,768]{1,0:T(8,128)(2,1)} %y_hbm.1), custom_call_target="tpu_custom_call" | custom-call | tf_op jit(solution)/shard_map/pallas_call | solution.py:548
  69.7 1.2 %copy.8 = f32[256]{0:T(256)} copy(f32[256]{0:T(256)} %bitcast.3) | data formatting | bytes 2048
  70.9 1.3 %copy.9 = f32[1024]{0:T(1024)} copy(f32[1024]{0:T(1024)} %bitcast.2) | data formatting | bytes 8192
